TPU v7x, 32 devices: a whole 2x2x4 slice. The times are simulated.
32 devices in a mesh: group: 2 (over y), expert: 4 (over z), dp: 4 (over x, core).
Axes of the slice: x: 2, y: 2, z: 4, core: 2. Of those that a mesh axis runs over, the one named last changes fastest.
Arguments:
- out_grad: bfloat16 [1024, 4096], P(('group', 'expert'), 'dp'), parts along dimension 0, may hold values from -6 to 6
- routes: int32 [1024, 8], P(('group', 'expert')), parts along dimension 0, may hold values from 0 to 15, all different within a row; in each aligned block of 128 rows (0 to 127, 128 to 255, ...) at most 128 rows name the same one
- route_prob: float32 [1024, 8], P(('group', 'expert')), parts along dimension 0, may hold values from 0.05 to 1
- down_weight: bfloat16 [16, 768, 4096], P('expert', None, 'dp'), may hold values from -0.21875 to 0.21875
- saved_hidden: bfloat16 [32, 512, 768], P(('group', 'expert'), 'dp'), parts along dimension 0, may hold values from -6 to 6
Outputs:
- scores: float32 [32, 768], P(('group', 'expert')), parts along dimension 0
- down_grad: bfloat16 [32, 768, 4096], P(('group', 'expert'), None, 'dp'), parts along dimension 0
There are 2 independent parts, one for each index of `group`. A program takes and returns all parts, laid end to end along the dimension named above; an argument that names none is the same for every part. Nothing has to cross between parts.
Inputs may be any that keep to these rules, and one draw needn't show every extreme that they name: `routes`: within the 128 tokens of each block no expert is named more than 128 times; each token names 8 different experts.
All inputs are finite; a program needn't handle non-finite values.
Results may differ from a plain program's by a relative error of at most 0.012.
Values may be sent and summed in bfloat16 or wider, within the bound.
No kernel may reach another device: no remote copies, remote signals or barrier semaphores. Data moves between devices by JAX's collectives and lax.ppermute only.
A program may use at most 128 MiB of HBM per device.

v0:
```python
import jax
import jax.numpy as jnp
from jax import lax
from jax.sharding import PartitionSpec as P


def shards(out_grad, routes, route_prob, down_weight, saved_hidden):
    owners = lax.axis_size("expert")
    dp_count = lax.axis_size("dp")
    tok_rows, columns = out_grad.shape
    fanout = routes.shape[1]
    local_experts = down_weight.shape[0]
    experts = local_experts * owners
    share_rows = saved_hidden.shape[1]
    slot_total = share_rows * dp_count
    capacity = slot_total // owners
    flat_routes = routes.reshape(-1)
    one_hot = (flat_routes[:, None] == jnp.arange(experts, dtype=jnp.int32)[None, :]).astype(
        jnp.int32
    )
    slot_rank = jnp.sum((jnp.cumsum(one_hot, axis=0) - 1) * one_hot, axis=1)
    position = (
        flat_routes % local_experts * slot_total
        + flat_routes // local_experts * capacity
        + slot_rank
    )
    routed = (out_grad[:, None, :].astype(jnp.float32) * route_prob[:, :, None]).astype(
        jnp.bfloat16
    )
    routed = routed.reshape(tok_rows * fanout, columns)
    outgoing = (
        jnp.zeros((local_experts * slot_total, columns), jnp.bfloat16).at[position].set(routed)
    )
    outgoing = outgoing.reshape(local_experts, owners, capacity, columns)
    incoming = lax.all_to_all(outgoing, "expert", split_axis=1, concat_axis=1, tiled=True).reshape(
        local_experts, slot_total, columns
    )
    partial_value = jnp.einsum(
        "esc,efc->esf", incoming, down_weight, preferred_element_type=jnp.float32
    )
    hidden_grad = lax.psum_scatter(
        partial_value.astype(jnp.bfloat16), "dp", scatter_dimension=1, tiled=True
    ).astype(jnp.float32)
    local_scores = jnp.sum((saved_hidden.astype(jnp.float32) * hidden_grad) ** 2, axis=1)
    scores = lax.psum(local_scores, "dp")
    gradient = jnp.einsum(
        "esf,esc->efc",
        lax.all_gather(saved_hidden, "dp", axis=1, tiled=True),
        incoming,
        preferred_element_type=jnp.float32,
    )
    return (scores, gradient.astype(jnp.bfloat16))


def solution(mesh):
    placed = (
        P(("group", "expert"), "dp"),
        P(("group", "expert"), None),
        P(("group", "expert"), None),
        P("expert", None, "dp"),
        P(("group", "expert"), "dp", None),
    )
    return jax.shard_map(
        shards,
        mesh=mesh,
        in_specs=placed,
        out_specs=(P(("group", "expert"), None), P(("group", "expert"), None, "dp")),
        check_vma=False,
    )
```

profile of v0, /device:TPU:0, one launch (start us, length us, event | category | flops | bytes accessed | tf_op | source)
XLA Modules:
  0.0 196.6 jit_solution(18423726145928119404)
XLA Ops:
  7.2 0.8 copy.28
  8.0 0.1 eq.31
  8.0 0.1 eq.27
  8.1 0.1 reshape.159
  8.2 4.5 %reduce-window.6 = s32[16,8,128]{2,1,0:T(8,128)S(1)} reduce-window(s32[16,8,128]{2,1,0:T(8,128)S(1)} %fusion.8, s32[]{:T(128)} %constant.36.clone.1), window={size=1x1x128 pad=0_0x0_0x127_0}, to_apply=%region_0.0 | reduce-window | flops 2080768 | bytes 131076 | tf_op jit(solution)/shard_map/reduce-window
  12.8 0.1 slice.8
  12.8 0.1 copy.31
  13.0 0.1 copy.32
  13.1 0.1 add_add_fusion
  13.2 0.8 copy.33
  14.0 0.1 mul.57
  14.1 1.0 convert_element_type.30
  15.1 8.4 %scatter_custom_fusion = bf16[2048,1024]{1,0:T(8,128)(2,1)} fusion(s32[1024]{0:T(1024)S(1)} %bitcast.35, f32[1024]{0:T(1024)S(1)} %mul.57, f32[128,1024]{1,0:T(8,128)S(1)} %convert_element_type.30, bf16[]{:T(256)} %constant.35.clone.1), kind=kCustom, calls=%fused_computation.5 | custom fusion | flops 2097152 | bytes 4722690 | tf_op jit(solution)/shard_map/scatter | solution.py:32
  23.5 4.9 %copy.34 = bf16[4,4,128,1024]{3,2,0,1:T(8,128)(2,1)} copy(bf16[4,4,128,1024]{3,2,1,0:T(8,128)(2,1)} %bitcast.29) | data formatting | bytes 8388608 | tf_op jit(solution)/shard_map/reshape | solution.py:34
  28.4 6.3 %all-to-all-start = ((bf16[4,4,128,1024]{3,2,0,1:T(8,128)(2,1)}), bf16[4,4,128,1024]{3,2,0,1:T(8,128)(2,1)}, u32[]{:S(2)}, u32[]{:S(2)}) async-start(bf16[4,4,128,1024]{3,2,0,1:T(8,128)(2,1)} %copy.34), calls=%async_computation | async-start | bytes 8388608 | tf_op jit(solution)/shard_map/all_to_all | solution.py:35
  34.7 0.0 all-gather.2.cloned.1.call-start
  34.7 0.7 all-gather.2.cloned.1.call-update
  35.4 0.2 reduce-scatter.2.cloned.1.call-start
  35.7 92.5 %all-to-all-done = bf16[4,4,128,1024]{3,2,0,1:T(8,128)(2,1)} async-done(((bf16[4,4,128,1024]{3,2,0,1:T(8,128)(2,1)}), bf16[4,4,128,1024]{3,2,0,1:T(8,128)(2,1)}, u32[]{:S(2)}, u32[]{:S(2)}) %all-to-all-start) | async-done | bytes 4194336 | tf_op jit(solution)/shard_map/all_to_all | solution.py:35
  128.2 2.6 %copy.35 = bf16[4,4,128,1024]{3,2,1,0:T(8,128)(2,1)S(1)} copy(bf16[4,4,128,1024]{3,2,0,1:T(8,128)(2,1)} %all-to-all-done) | data formatting | bytes 8388608 | tf_op jit(solution)/shard_map/all_to_all | solution.py:35
  130.8 0.0 copy-start
  130.8 2.0 %copy-done = bf16[4,4,128,1024]{3,2,1,0:T(8,128)(2,1)} copy-done((bf16[4,4,128,1024]{3,2,1,0:T(8,128)(2,1)}, bf16[4,4,128,1024]{3,2,1,0:T(8,128)(2,1)S(1)}, u32[]{:S(2)}) %copy-start) | copy-done | bytes 4194328
  132.8 7.6 %convolution_convert_fusion = bf16[4,512,768]{2,1,0:T(8,128)(2,1)} fusion(bf16[4,512,1024]{2,1,0:T(8,128)(2,1)S(1)} %bitcast.30, bf16[4,768,1024]{2,1,0:T(8,128)(2,1)} %param.8), kind=kOutput, calls=%fused_computation.4 | convolution fusion | flops 3222798336 | bytes 13631488 | tf_op jit(solution)/shard_map/esc,efc->esf/dot_general | solution.py:38
  140.4 0.0 reduce-scatter.2.cloned.1.call-update
  140.4 0.0 all-gather.2.cloned.1.call-done
  140.5 9.4 %convert_bitcast_fusion = bf16[4,768,1024]{1,2,0:T(8,128)(2,1)} fusion(bf16[4,512,1024]{2,1,0:T(8,128)(2,1)} %bitcast.31, bf16[4,512,768]{2,1,0:T(8,128)(2,1)} %all-gather.2.cloned.1.call-done), kind=kOutput, calls=%fused_computation.1 | convolution fusion | flops 3224371200 | bytes 13631488 | tf_op jit(solution)/shard_map/esf,esc->efc/dot_general | solution.py:46
  149.9 0.0 copy-start.1
  149.9 8.7 %copy.37 = bf16[4,768,1024]{2,1,0:T(8,128)(2,1)} copy(bf16[4,768,1024]{1,2,0:T(8,128)(2,1)} %convert_bitcast_fusion) | data formatting | bytes 12582912
  158.6 19.0 %reduce-scatter.2.cloned.1.call-done = bf16[4,128,768]{2,1,0:T(8,128)(2,1)} async-done(((bf16[4,512,768]{2,1,0:T(8,128)(2,1)}), bf16[4,128,768]{2,1,0:T(8,128)(2,1)}) %reduce-scatter.2.cloned.1.call-update) | async-done | bytes 786448 | tf_op jit(solution)/shard_map/reduce_scatter | solution.py:41
  177.7 0.0 copy-done.1
  177.7 1.4 multiply_reduce_fusion
  179.1 10.7 %psum.7 = f32[4,768]{1,0:T(4,128)} all-reduce(f32[4,768]{1,0:T(4,128)S(1)} %multiply_reduce_fusion), channel_id=1, replica_groups=mesh['group'=2,'expert'=4,'dp'=4] {'dp'}, use_global_device_ids=true, to_apply=%region_6.7 | all-reduce | flops 3072 | bytes 24576 | tf_op jit(solution)/shard_map/psum | solution.py:45
  (5 shorter events, 0.1 us)
Async XLA Ops:
  28.4 99.8 %all-to-all-start = ((bf16[4,4,128,1024]{3,2,0,1:T(8,128)(2,1)}), bf16[4,4,128,1024]{3,2,0,1:T(8,128)(2,1)}, u32[]{:S(2)}, u32[]{:S(2)}) async-start(bf16[4,4,128,1024]{3,2,0,1:T(8,128)(2,1)} %copy.34), calls=%async_computation | async-start | bytes 8388608 | tf_op jit(solution)/shard_map/all_to_all | solution.py:35
  34.7 105.8 %all-gather.2.cloned.1.call-start = ((), (), s32[]{:S(2)}) async-start(), calls=%async_computation.3 | async-start | bytes 3932160 | tf_op jit(solution)/shard_map/all_gather | solution.py:48
  35.4 142.2 %reduce-scatter.2.cloned.1.call-start = ((), (), s32[]{:S(2)}) async-start(), calls=%async_computation.2 | async-start | bytes 3932160 | tf_op jit(solution)/shard_map/reduce_scatter | solution.py:41
  130.8 2.0 %copy-start = (bf16[4,4,128,1024]{3,2,1,0:T(8,128)(2,1)}, bf16[4,4,128,1024]{3,2,1,0:T(8,128)(2,1)S(1)}, u32[]{:S(2)}) copy-start(bf16[4,4,128,1024]{3,2,1,0:T(8,128)(2,1)S(1)} %copy.35) | copy-start | bytes 12582916
  149.9 27.8 %copy-start.1 = (bf16[4,128,768]{2,1,0:T(8,128)(2,1)S(1)}, bf16[4,128,768]{2,1,0:T(8,128)(2,1)}, u32[]{:S(2)}) copy-start(bf16[4,128,768]{2,1,0:T(8,128)(2,1)} %param.9) | copy-start | bytes 2359300
Sparse Core Ops, SparseCore 0:
  37.1 29.9 all-gather.1
  140.6 37.0 reduce-scatter.1
where the time goes:
time: 197 us
  waiting for transfers between devices  112 us (57%)
  local copies, waits for them, and re-layouts  20.5 us (10%)
  matrix products  17 us (9%)
  other arithmetic  15.5 us (8%)
  between operations  14.1 us (7%)
  blocking collectives  10.7 us (5%)
  starting transfers between devices  6.54 us (3%)
    all_to_all x1, waiting for transfers between devices, shards(): lax.all_to_all(outgoing, 'expert', split_axis=1, concat_axis=1, tiled=True)  92.5 us
    reduce_scatter x1, waiting for transfers between devices, shards(): lax.psum_scatter(partial_value.astype(jnp.bfloat16), 'dp', scatter_dimens...  19 us
    unnamed x7, local copies, waits for them, and re-layouts  12.3 us
    psum x1, blocking collectives, shards(): scores = lax.psum(local_scores, 'dp')  10.7 us
    dot_general x1, matrix products, shards(): jnp.einsum('esf,esc->efc', lax.all_gather(saved_hidden, 'dp', axis=1, til...  9.42 us
    scatter x1, other arithmetic, shards(): jnp.zeros((local_experts * slot_total, columns), jnp.bfloat16).at[position]  8.37 us
    dot_general x1, matrix products, shards(): jnp.einsum('esc,efc->esf', incoming, down_weight, preferred_element_type=...  7.6 us
    all_to_all x1, starting transfers between devices, shards(): lax.all_to_all(outgoing, 'expert', split_axis=1, concat_axis=1, tiled=True)  6.32 us
  transfers between devices with their start and end apart: 3, of which 2 were waited for; matrix products, arithmetic and copies ran while one was open for 14% of the time, Pallas kernels for 0%

commit v1 on v0

v1 whole, which is shorter than its diff:
```python
import functools

import jax
import jax.numpy as jnp
from jax import lax
from jax.experimental import pallas as pl
from jax.experimental.pallas import tpu as pltpu
from jax.sharding import PartitionSpec as P

CORES = 2


def rotate(value, axis, step):
    count = lax.axis_size(axis)
    return lax.ppermute(value, axis, [(i, (i + step) % count) for i in range(count)])


def dp_shift(value, chip_step, core_flip):
    count = lax.axis_size("dp")
    chips = count // CORES
    pairs = []
    for chip in range(chips):
        for core in range(CORES):
            target = (chip - chip_step) % chips
            pairs.append((chip * CORES + core, target * CORES + (core ^ core_flip)))
    return lax.ppermute(value, "dp", pairs)


def ring_gather(block):
    owners = lax.axis_size("expert")
    rows = block.shape[0]
    got = {0: [block]}
    ahead = behind = block
    for step in range(1, owners // 2):
        behind = rotate(behind, "expert", 1)
        ahead = rotate(ahead, "expert", -1)
        got[owners - step] = [behind]
        got[step] = [ahead]
    half = rows // 2
    top = rotate(ahead[:half], "expert", -1)
    low = rotate(behind[half:], "expert", 1)
    got[owners // 2] = [top, low]
    return [got[r] for r in range(owners)]


def dispatch_body(pieces, first, order, routes, probs, *refs):
    total = sum(pieces)
    blocks, (weight, routed, keep, send, table) = refs[:total], refs[total:]
    owners, capacity = routes.shape[0], routed.shape[1] // routes.shape[0]
    tokens = routes.shape[2]

    at = 0
    for r, count in enumerate(pieces):
        row = 0
        for _ in range(count):
            part = blocks[at]
            table[r, row : row + part.shape[0], :] = part[...]
            row += part.shape[0]
            at += 1

    expert = order[owners] + first + pl.program_id(0)
    named, weights = [], []
    for r in range(owners):
        hit = routes[r] == expert
        named.append(jnp.max(hit.astype(jnp.float32), axis=0, keepdims=True))
        weights.append(jnp.sum(jnp.where(hit, probs[r], 0.0), axis=0, keepdims=True))
    named = jnp.concatenate(named, axis=0)
    before = (
        lax.broadcasted_iota(jnp.int32, (tokens, tokens), 0)
        < lax.broadcasted_iota(jnp.int32, (tokens, tokens), 1)
    )
    rank = jnp.dot(
        named.astype(jnp.bfloat16),
        before.astype(jnp.float32).astype(jnp.bfloat16),
        preferred_element_type=jnp.float32,
    )
    place = jnp.where(named > 0.0, rank, -1.0).astype(jnp.int32)
    slots = lax.broadcasted_iota(jnp.int32, (capacity, tokens), 0)
    for r in range(owners):
        taken = slots == place[r : r + 1, :]
        rows = jnp.dot(
            taken.astype(jnp.float32).astype(jnp.bfloat16),
            table[r],
            preferred_element_type=jnp.float32,
        )
        scale = jnp.sum(jnp.where(taken, weights[r], 0.0), axis=1, keepdims=True)
        position = pl.multiple_of(order[r] * capacity, capacity)
        routed[0, pl.ds(position, capacity), :] = (rows * scale).astype(jnp.bfloat16)
    partial_value = lax.dot_general(
        routed[0], weight[0], (((1,), (1,)), ((), ())), preferred_element_type=jnp.float32
    ).astype(jnp.bfloat16)
    half = partial_value.shape[0] // CORES
    keep[0] = partial_value[:half]
    send[0] = partial_value[half:]


def dispatch(order, routes, probs, blocks, down_weight, first, count, capacity):
    owners, fanout, tokens = routes.shape
    _, hidden, columns = down_weight.shape
    slots = owners * capacity
    flat = [part for parts in blocks for part in parts]
    whole = lambda shape: pl.BlockSpec(shape, lambda e, order: (0,) * len(shape))
    by_expert = lambda shape: pl.BlockSpec((1,) + shape, lambda e, order: (e, 0, 0))
    return pl.pallas_call(
        functools.partial(dispatch_body, [len(parts) for parts in blocks], first),
        grid_spec=pltpu.PrefetchScalarGridSpec(
            num_scalar_prefetch=1,
            grid=(count,),
            in_specs=[whole(routes.shape), whole(probs.shape)]
            + [whole(part.shape) for part in flat]
            + [pl.BlockSpec((1, hidden, columns), lambda e, order: (first + e, 0, 0))],
            out_specs=[
                by_expert((slots, columns)),
                by_expert((slots // CORES, hidden)),
                by_expert((slots // CORES, hidden)),
            ],
            scratch_shapes=[pltpu.VMEM((owners, tokens, columns), jnp.bfloat16)],
        ),
        out_shape=[
            jax.ShapeDtypeStruct((count, slots, columns), jnp.bfloat16),
            jax.ShapeDtypeStruct((count, slots // CORES, hidden), jnp.bfloat16),
            jax.ShapeDtypeStruct((count, slots // CORES, hidden), jnp.bfloat16),
        ],
        compiler_params=pltpu.CompilerParams(vmem_limit_bytes=40 * 2**20),
        cost_estimate=pl.CostEstimate(
            flops=2 * count * slots * columns * (hidden + tokens),
            bytes_accessed=2 * count * (hidden * columns + slots * (columns + hidden)),
            transcendentals=0,
        ),
    )(order, routes, probs, *flat, down_weight)


def gradient_body(*refs):
    saved, (routed, out) = refs[:-2], refs[-2:]
    whole = jnp.concatenate([part[0] for part in saved], axis=0)
    out[0] = lax.dot_general(
        whole, routed[0], (((0,), (0,)), ((), ())), preferred_element_type=jnp.float32
    ).astype(jnp.bfloat16)


def gradient_of(saved, routed):
    experts, slots, columns = routed.shape
    hidden = saved[0].shape[2]
    by_expert = lambda shape: pl.BlockSpec((1,) + shape, lambda e: (e, 0, 0))
    return pl.pallas_call(
        gradient_body,
        grid=(experts,),
        in_specs=[by_expert(part.shape[1:]) for part in saved] + [by_expert((slots, columns))],
        out_specs=by_expert((hidden, columns)),
        out_shape=jax.ShapeDtypeStruct((experts, hidden, columns), jnp.bfloat16),
        compiler_params=pltpu.CompilerParams(vmem_limit_bytes=40 * 2**20),
        cost_estimate=pl.CostEstimate(
            flops=2 * experts * slots * columns * hidden,
            bytes_accessed=2 * experts * (hidden * columns + slots * (columns + hidden)),
            transcendentals=0,
        ),
    )(*saved, routed)


def shards(out_grad, routes, route_prob, down_weight, saved_hidden):
    owners = lax.axis_size("expert")
    dp_count = lax.axis_size("dp")
    chips = dp_count // CORES
    local_experts, share_rows, _ = saved_hidden.shape
    capacity = share_rows * dp_count // owners
    assert capacity == share_rows
    mine, index = lax.axis_index("expert"), lax.axis_index("dp")
    chip, core = index // CORES, index % CORES

    source = (mine + jnp.arange(owners, dtype=jnp.int32)) % owners
    position = (source % CORES != core) * chips + (source // CORES - chip) % chips
    order = jnp.concatenate([position, (mine * local_experts)[None]]).astype(jnp.int32)

    saved = [saved_hidden]
    for step in range(1, chips):
        saved.append(dp_shift(saved_hidden, step, 0))
    saved = saved + [dp_shift(part, 0, 1) for part in saved]

    route_rows = [routes.T] + [rotate(routes.T, "expert", -r) for r in range(1, owners)]
    prob_rows = [route_prob.T] + [rotate(route_prob.T, "expert", -r) for r in range(1, owners)]
    route_rows, prob_rows = jnp.stack(route_rows), jnp.stack(prob_rows)
    blocks = ring_gather(out_grad)

    routed, squares = [], []
    for e in range(local_experts):
        rows, keep, send = dispatch(
            order, route_rows, prob_rows, blocks, down_weight, e, 1, capacity
        )
        routed.append(rows)
        other = dp_shift(send, 0, 1)
        total = keep.astype(jnp.float32) + other.astype(jnp.float32)
        hidden_grad = total[0, :share_rows]
        for step in range(1, chips):
            leaving = total[0, step * share_rows : (step + 1) * share_rows].astype(jnp.bfloat16)
            hidden_grad = hidden_grad + dp_shift(leaving, -step, 0).astype(jnp.float32)
        squares.append(jnp.sum((saved_hidden[e].astype(jnp.float32) * hidden_grad) ** 2, axis=0))
    local = jnp.stack(squares)
    local = local + dp_shift(local, 0, 1)
    parts = [local] + [dp_shift(local, step, 0) for step in range(1, chips)]
    if chips > 2:
        parts = jnp.roll(jnp.stack(parts), chip, axis=0)
        scores = jnp.sum(parts, axis=0)
    else:
        scores = sum(parts)

    gradient = gradient_of(saved, jnp.concatenate(routed, axis=0))
    return (scores, gradient)


def solution(mesh):
    placed = (
        P(("group", "expert"), "dp"),
        P(("group", "expert"), None),
        P(("group", "expert"), None),
        P("expert", None, "dp"),
        P(("group", "expert"), "dp", None),
    )
    return jax.shard_map(
        shards,
        mesh=mesh,
        in_specs=placed,
        out_specs=(P(("group", "expert"), None), P(("group", "expert"), None, "dp")),
        check_vma=False,
    )
```

time: 197 us -> 83.3 us (0.42)
  waiting for transfers between devices: 112 us -> 32.4 us
  starting transfers between devices: 6.54 us -> 28.9 us
  matrix products: 17 us -> 0 us
  local copies, waits for them, and re-layouts: 20.5 us -> 3.86 us
  Pallas kernels: 0 us -> 13.7 us
  between operations: 14.1 us -> 0.81 us
  other arithmetic: 15.5 us -> 3.33 us
  blocking collectives: 10.7 us -> 0 us
    all_to_all x1 -> x0, waiting for transfers between devices: 92.5 us -> none  [shards(): lax.all_to_all(outgoing, 'expert', split_axis=1, concat_axis=1, tiled=True)]
    ppermute x0 -> x23, waiting for transfers between devices: none -> 32.4 us  [the longest x13 25.6 us: dp_shift(): return lax.ppermute(value, 'dp', pairs)]
    ppermute x0 -> x23, starting transfers between devices: none -> 28.9 us  [the longest x10 19.9 us: rotate(): lax.ppermute(value, axis, [(i, (i + step) % count) for i in range(count)])]
    reduce_scatter x1 -> x0, waiting for transfers between devices: 19 us -> none  [shards(): lax.psum_scatter(partial_value.astype(jnp.bfloat16), 'dp', scatter_dimens...]
    dot_general x2 -> x0, matrix products: 17 us -> none  [the longest x1 9.42 us: shards(): jnp.einsum('esf,esc->efc', lax.all_gather(saved_hidden, 'dp', axis=1, til...]
    pallas_call x0 -> x5, Pallas kernels: none -> 13.7 us  [the longest x4 8.34 us: dispatch(): pl.pallas_call(functools.partial(dispatch_body, [len(parts) for parts in...]
    psum x1 -> x0, blocking collectives: 10.7 us -> none  [shards(): scores = lax.psum(local_scores, 'dp')]
    unnamed x7 -> x6, local copies, waits for them, and re-layouts: 12.3 us -> 3.74 us
  transfers between devices with their start and end apart: 3 -> 23, of which waited for: 2 -> 9; matrix products, arithmetic and copies ran while one was open for 14% -> 4% of each run, Pallas kernels for 0% -> 8%
where the time goes in v1:
time: 83.3 us; the launch traced here: 83 us
  waiting for transfers between devices  32.4 us (39%)
  starting transfers between devices  28.9 us (35%)
  Pallas kernels  13.7 us (16%)
  local copies, waits for them, and re-layouts  3.86 us (5%)
  other arithmetic  3.33 us (4%)
    ppermute x13, waiting for transfers between devices, dp_shift(): return lax.ppermute(value, 'dp', pairs)  25.6 us
    ppermute x10, starting transfers between devices, rotate(): lax.ppermute(value, axis, [(i, (i + step) % count) for i in range(count)])  19.9 us
    ppermute x13, starting transfers between devices, dp_shift(): return lax.ppermute(value, 'dp', pairs)  9 us
    pallas_call x4, Pallas kernels, dispatch(): pl.pallas_call(functools.partial(dispatch_body, [len(parts) for parts in...  8.34 us
    ppermute x10, waiting for transfers between devices, rotate(): lax.ppermute(value, axis, [(i, (i + step) % count) for i in range(count)])  6.84 us
    pallas_call x1, Pallas kernels, gradient_of(): pl.pallas_call(gradient_body, grid=(experts,), in_specs=[by_expert(part.s...  5.36 us
    unnamed x6, local copies, waits for them, and re-layouts  3.74 us
  transfers between devices with their start and end apart: 23, of which 9 were waited for; matrix products, arithmetic and copies ran while one was open for 4% of the time, Pallas kernels for 8%

profile of v1, /device:TPU:0, one launch (start us, length us, event | category | flops | bytes accessed | tf_op | source)
XLA Modules:
  0.0 83.0 jit_solution(10873443184472379047)
XLA Ops:
  0.6 3.1 %collective-permute-start.8 = (bf16[128,1024]{1,0:T(8,128)(2,1)}, bf16[128,1024]{1,0:T(8,128)(2,1)S(1)}, u32[]{:S(2)}, u32[]{:S(2)}) collective-permute-start(bf16[128,1024]{1,0:T(8,128)(2,1)} %refs_0_.8), channel_id=1, source_target_pairs={{0,4},{4,8},{8,12},{12,0},{1,5},{5,9},{9,13},{13,1},{2,6},{6,10},{... | collective-permute-start | bytes 786440 | tf_op jit(solution)/shard_map/ppermute | solution.py:15
  3.7 2.1 %collective-permute-start.6 = (bf16[128,1024]{1,0:T(8,128)(2,1)}, bf16[128,1024]{1,0:T(8,128)(2,1)S(1)}, u32[]{:S(2)}, u32[]{:S(2)}) collective-permute-start(bf16[128,1024]{1,0:T(8,128)(2,1)} %refs_0_.8), channel_id=1, source_target_pairs={{0,12},{4,0},{8,4},{12,8},{1,13},{5,1},{9,5},{13,9},{2,14},{6,2},{... | collective-permute-start | bytes 786440 | tf_op jit(solution)/shard_map/ppermute | solution.py:15
  5.8 0.9 %collective-permute-start.1 = (s32[8,128]{1,0:T(8,128)}, s32[8,128]{1,0:T(8,128)S(1)}, u32[]{:S(2)}, u32[]{:S(2)}) collective-permute-start(s32[8,128]{1,0:T(8,128)} %bitcast.73), channel_id=1, source_target_pairs={{0,8},{4,12},{8,0},{12,4},{1,9},{5,13},{9,1},{13,5},{2,10},{6,14},... | collective-permute-start | bytes 12296 | tf_op jit(solution)/shard_map/ppermute | solution.py:15
  6.7 1.3 %collective-permute-start = (s32[8,128]{1,0:T(8,128)}, s32[8,128]{1,0:T(8,128)S(1)}, u32[]{:S(2)}, u32[]{:S(2)}) collective-permute-start(s32[8,128]{1,0:T(8,128)} %bitcast.74), channel_id=1, source_target_pairs={{0,12},{4,0},{8,4},{12,8},{1,13},{5,1},{9,5},{13,9},{2,14},{6,2},{... | collective-permute-start | bytes 12296 | tf_op jit(solution)/shard_map/ppermute | solution.py:15
  8.1 0.7 collective-permute-start.2
  8.8 0.1 pad_add_fusion.1.order
  8.9 4.2 %collective-permute-done.8.refs_4_ = bf16[128,1024]{1,0:T(8,128)(2,1)S(1)} collective-permute-done((bf16[128,1024]{1,0:T(8,128)(2,1)}, bf16[128,1024]{1,0:T(8,128)(2,1)S(1)}, u32[]{:S(2)}, u32[]{:S(2)}) %collective-permute-start.8) | collective-permute-done | bytes 262176 | tf_op jit(solution)/shard_map/ppermute | solution.py:15
  13.1 5.8 %collective-permute-start.4 = (f32[8,128]{1,0:T(8,128)}, f32[8,128]{1,0:T(8,128)S(1)}, u32[]{:S(2)}, u32[]{:S(2)}) collective-permute-start(f32[8,128]{1,0:T(8,128)} %bitcast.77), channel_id=1, source_target_pairs={{0,8},{4,12},{8,0},{12,4},{1,9},{5,13},{9,1},{13,5},{2,10},{6,14},... | collective-permute-start | bytes 12296 | tf_op jit(solution)/shard_map/ppermute | solution.py:15
  19.0 0.9 %collective-permute-start.3 = (f32[8,128]{1,0:T(8,128)}, f32[8,128]{1,0:T(8,128)S(1)}, u32[]{:S(2)}, u32[]{:S(2)}) collective-permute-start(f32[8,128]{1,0:T(8,128)} %bitcast.78), channel_id=1, source_target_pairs={{0,12},{4,0},{8,4},{12,8},{1,13},{5,1},{9,5},{13,9},{2,14},{6,2},{... | collective-permute-start | bytes 12296 | tf_op jit(solution)/shard_map/ppermute | solution.py:15
  19.9 1.2 %collective-permute-start.5 = (f32[8,128]{1,0:T(8,128)}, f32[8,128]{1,0:T(8,128)S(1)}, u32[]{:S(2)}, u32[]{:S(2)}) collective-permute-start(f32[8,128]{1,0:T(8,128)} %bitcast.79), channel_id=1, source_target_pairs={{0,4},{4,8},{8,12},{12,0},{1,5},{5,9},{9,13},{13,1},{2,6},{6,10},{... | collective-permute-start | bytes 12296 | tf_op jit(solution)/shard_map/ppermute | solution.py:15
  21.1 1.4 %collective-permute-start.9 = (bf16[64,1024]{1,0:T(8,128)(2,1)S(1)}, bf16[64,1024]{1,0:T(8,128)(2,1)S(1)}, u32[]{:S(2)}, u32[]{:S(2)}) collective-permute-start(bf16[64,1024]{1,0:T(8,128)(2,1)S(1)} %slice.61), channel_id=1, source_target_pairs={{0,4},{4,8},{8,12},{12,0},{1,5},{5,9},{9,13},{13,1},{2,6},{6,10},{... | collective-permute-start | bytes 393224 | tf_op jit(solution)/shard_map/ppermute | solution.py:15
  22.5 2.4 %collective-permute-start.7 = (bf16[64,1024]{1,0:T(8,128)(2,1)S(1)}, bf16[64,1024]{1,0:T(8,128)(2,1)S(1)}, u32[]{:S(2)}, u32[]{:S(2)}) collective-permute-start(bf16[64,1024]{1,0:T(8,128)(2,1)S(1)} %slice.60), channel_id=1, source_target_pairs={{0,12},{4,0},{8,4},{12,8},{1,13},{5,1},{9,5},{13,9},{2,14},{6,2},{... | collective-permute-start | bytes 393224 | tf_op jit(solution)/shard_map/ppermute | solution.py:15
  24.9 0.7 pad_add_fusion.routes
  25.7 0.7 pad_maximum_fusion.1.probs
  26.4 1.7 %collective-permute-done.9.refs_3_ = bf16[64,1024]{1,0:T(8,128)(2,1)S(1)} collective-permute-done((bf16[64,1024]{1,0:T(8,128)(2,1)S(1)}, bf16[64,1024]{1,0:T(8,128)(2,1)S(1)}, u32[]{:S(2)}, u32[]{:S(2)}) %collective-permute-start.9) | collective-permute-done | bytes 131104 | tf_op jit(solution)/shard_map/ppermute | solution.py:15
  28.0 0.9 %collective-permute-done.7.refs_2_ = bf16[64,1024]{1,0:T(8,128)(2,1)S(1)} collective-permute-done((bf16[64,1024]{1,0:T(8,128)(2,1)S(1)}, bf16[64,1024]{1,0:T(8,128)(2,1)S(1)}, u32[]{:S(2)}, u32[]{:S(2)}) %collective-permute-start.7) | collective-permute-done | bytes 131104 | tf_op jit(solution)/shard_map/ppermute | solution.py:15
  28.9 2.8 %copy-done = bf16[4,768,1024]{2,1,0:T(8,128)(2,1)S(1)} copy-done((bf16[4,768,1024]{2,1,0:T(8,128)(2,1)S(1)}, bf16[4,768,1024]{2,1,0:T(8,128)(2,1)}, u32[]{:S(2)}) %copy-start) | copy-done | bytes 6291480
  31.7 0.9 %copy-done.1 = bf16[128,1024]{1,0:T(8,128)(2,1)S(1)} copy-done((bf16[128,1024]{1,0:T(8,128)(2,1)S(1)}, bf16[128,1024]{1,0:T(8,128)(2,1)}, u32[]{:S(2)}) %copy-start.1) | copy-done | bytes 262168
  32.7 2.1 %shard_map.71 = (bf16[1,512,1024]{2,1,0:T(8,128)(2,1)S(1)}, bf16[1,256,768]{2,1,0:T(8,128)(2,1)S(1)}, bf16[1,256,768]{2,1,0:T(8,128)(2,1)S(1)}) custom-call(s32[5]{0:T(128)S(1)} %pad_add_fusion.1.order, s32[4,8,128]{2,1,0:T(8,128)S(1)} %pad_add_fusion.routes, f32[4,8,128]{2,1,0:T(8,128)S(1)} %pad_maximum_fusion.1.probs, bf16[128,1024]{1,0:T(8,128)(2,1)S(1)} %copy-done.1, ...), custom_call_target="tpu_custom_call" | custom-call | flops 939524096 | bytes 3407872 | tf_op jit(solution)/shard_map/pallas_call | solution.py:104
  34.8 1.6 %collective-permute-start.20 = (bf16[4,128,768]{2,1,0:T(8,128)(2,1)S(1)}, bf16[4,128,768]{2,1,0:T(8,128)(2,1)S(1)}, u32[]{:S(2)}, u32[]{:S(2)}) collective-permute-start(bf16[4,128,768]{2,1,0:T(8,128)(2,1)S(1)} %copy-done.2), channel_id=1, source_target_pairs={{0,2},{1,3},{2,0},{3,1},{4,6},{5,7},{6,4},{7,5},{8,10},{9,11},{10,... | collective-permute-start | bytes 2359304 | tf_op jit(solution)/shard_map/ppermute | solution.py:26
  36.4 2.1 %shard_map.70 = (bf16[1,512,1024]{2,1,0:T(8,128)(2,1)S(1)}, bf16[1,256,768]{2,1,0:T(8,128)(2,1)S(1)}, bf16[1,256,768]{2,1,0:T(8,128)(2,1)S(1)}) custom-call(s32[5]{0:T(128)S(1)} %pad_add_fusion.1.order, s32[4,8,128]{2,1,0:T(8,128)S(1)} %pad_add_fusion.routes, f32[4,8,128]{2,1,0:T(8,128)S(1)} %pad_maximum_fusion.1.probs, bf16[128,1024]{1,0:T(8,128)(2,1)S(1)} %copy-done.1, ...), custom_call_target="tpu_custom_call" | custom-call | flops 939524096 | bytes 3407872 | tf_op jit(solution)/shard_map/pallas_call | solution.py:104
  38.5 0.2 collective-permute-start.14
  38.7 2.1 %shard_map.69 = (bf16[1,512,1024]{2,1,0:T(8,128)(2,1)S(1)}, bf16[1,256,768]{2,1,0:T(8,128)(2,1)S(1)}, bf16[1,256,768]{2,1,0:T(8,128)(2,1)S(1)}) custom-call(s32[5]{0:T(128)S(1)} %pad_add_fusion.1.order, s32[4,8,128]{2,1,0:T(8,128)S(1)} %pad_add_fusion.routes, f32[4,8,128]{2,1,0:T(8,128)S(1)} %pad_maximum_fusion.1.probs, bf16[128,1024]{1,0:T(8,128)(2,1)S(1)} %copy-done.1, ...), custom_call_target="tpu_custom_call" | custom-call | flops 939524096 | bytes 3407872 | tf_op jit(solution)/shard_map/pallas_call | solution.py:104
  40.8 0.4 collective-permute-start.12
  41.2 2.1 %shard_map.68 = (bf16[1,512,1024]{2,1,0:T(8,128)(2,1)S(1)}, bf16[1,256,768]{2,1,0:T(8,128)(2,1)S(1)}, bf16[1,256,768]{2,1,0:T(8,128)(2,1)S(1)}) custom-call(s32[5]{0:T(128)S(1)} %pad_add_fusion.1.order, s32[4,8,128]{2,1,0:T(8,128)S(1)} %pad_add_fusion.routes, f32[4,8,128]{2,1,0:T(8,128)S(1)} %pad_maximum_fusion.1.probs, bf16[128,1024]{1,0:T(8,128)(2,1)S(1)} %copy-done.1, ...), custom_call_target="tpu_custom_call" | custom-call | flops 939524096 | bytes 3407872 | tf_op jit(solution)/shard_map/pallas_call | solution.py:104
  43.3 0.2 collective-permute-start.10
  43.5 0.1 convert_add_fusion
  43.6 0.6 collective-permute-start.17
  44.2 0.1 convert_add_fusion.1
  44.3 1.6 %collective-permute-start.15 = (bf16[128,768]{1,0:T(8,128)(2,1)S(1)}, bf16[128,768]{1,0:T(8,128)(2,1)S(1)}, u32[]{:S(2)}, u32[]{:S(2)}) collective-permute-start(bf16[128,768]{1,0:T(8,128)(2,1)S(1)} %fusion.18), channel_id=1, source_target_pairs={{0,2},{1,3},{2,0},{3,1},{4,6},{5,7},{6,4},{7,5},{8,10},{9,11},{10,... | collective-permute-start | bytes 589832 | tf_op jit(solution)/shard_map/ppermute | solution.py:26
  45.9 0.1 convert_add_fusion.2
  46.0 0.6 collective-permute-start.13
  46.6 0.1 convert_add_fusion.3
  46.7 1.6 %collective-permute-start.11 = (bf16[128,768]{1,0:T(8,128)(2,1)S(1)}, bf16[128,768]{1,0:T(8,128)(2,1)S(1)}, u32[]{:S(2)}, u32[]{:S(2)}) collective-permute-start(bf16[128,768]{1,0:T(8,128)(2,1)S(1)} %fusion.16), channel_id=1, source_target_pairs={{0,2},{1,3},{2,0},{3,1},{4,6},{5,7},{6,4},{7,5},{8,10},{9,11},{10,... | collective-permute-start | bytes 589832 | tf_op jit(solution)/shard_map/ppermute | solution.py:26
  48.3 11.2 %collective-permute-done.17 = bf16[128,768]{1,0:T(8,128)(2,1)S(1)} collective-permute-done((bf16[128,768]{1,0:T(8,128)(2,1)S(1)}, bf16[128,768]{1,0:T(8,128)(2,1)S(1)}, u32[]{:S(2)}, u32[]{:S(2)}) %collective-permute-start.17) | collective-permute-done | bytes 196640 | tf_op jit(solution)/shard_map/ppermute | solution.py:26
  59.5 4.2 %collective-permute-done.15 = bf16[128,768]{1,0:T(8,128)(2,1)S(1)} collective-permute-done((bf16[128,768]{1,0:T(8,128)(2,1)S(1)}, bf16[128,768]{1,0:T(8,128)(2,1)S(1)}, u32[]{:S(2)}, u32[]{:S(2)}) %collective-permute-start.15) | collective-permute-done | bytes 196640 | tf_op jit(solution)/shard_map/ppermute | solution.py:26
  63.7 4.2 %collective-permute-done.13 = bf16[128,768]{1,0:T(8,128)(2,1)S(1)} collective-permute-done((bf16[128,768]{1,0:T(8,128)(2,1)S(1)}, bf16[128,768]{1,0:T(8,128)(2,1)S(1)}, u32[]{:S(2)}, u32[]{:S(2)}) %collective-permute-start.13) | collective-permute-done | bytes 196640 | tf_op jit(solution)/shard_map/ppermute | solution.py:26
  67.9 3.8 %collective-permute-done.11 = bf16[128,768]{1,0:T(8,128)(2,1)S(1)} collective-permute-done((bf16[128,768]{1,0:T(8,128)(2,1)S(1)}, bf16[128,768]{1,0:T(8,128)(2,1)S(1)}, u32[]{:S(2)}, u32[]{:S(2)}) %collective-permute-start.11) | collective-permute-done | bytes 196640 | tf_op jit(solution)/shard_map/ppermute | solution.py:26
  71.6 0.3 fusion.15
  72.0 0.1 collective-permute-start.18
  72.1 0.5 collective-permute-start.21
  72.6 0.1 collective-permute-start.22
  72.7 0.6 collective-permute-done.18
  73.3 1.6 %collective-permute-start.19 = (f32[4,768]{1,0:T(4,128)S(1)}, f32[4,768]{1,0:T(4,128)S(1)}, u32[]{:S(2)}, u32[]{:S(2)}) collective-permute-start(f32[4,768]{1,0:T(4,128)S(1)} %fusion.23), channel_id=1, source_target_pairs={{0,2},{1,3},{2,0},{3,1},{4,6},{5,7},{6,4},{7,5},{8,10},{9,11},{10,... | collective-permute-start | bytes 36872 | tf_op jit(solution)/shard_map/ppermute | solution.py:26
  74.9 0.5 pad_maximum_fusion.refs_4_
  75.4 1.7 %collective-permute-done.19 = f32[4,768]{1,0:T(4,128)S(1)} collective-permute-done((f32[4,768]{1,0:T(4,128)S(1)}, f32[4,768]{1,0:T(4,128)S(1)}, u32[]{:S(2)}, u32[]{:S(2)}) %collective-permute-start.19) | collective-permute-done | bytes 12320 | tf_op jit(solution)/shard_map/ppermute | solution.py:26
  77.1 0.6 fusion.24
  77.7 5.4 %shard_map.72 = bf16[4,768,1024]{2,1,0:T(8,128)(2,1)} custom-call(bf16[4,128,768]{2,1,0:T(8,128)(2,1)S(1)} %copy-done.2, bf16[4,128,768]{2,1,0:T(8,128)(2,1)S(1)} %collective-permute-done.20.refs_1_, bf16[4,128,768]{2,1,0:T(8,128)(2,1)S(1)} %collective-permute-done.21.refs_2_, bf16[4,128,768]{2,1,0:T(8,128)(2,1)S(1)} %collective-permute-done.22.refs_3_, ...), custom_call_target="tpu_custom_call" | custom-call | flops 3221225472 | bytes 13631488 | tf_op jit(solution)/shard_map/pallas_call | solution.py:145
  (32 shorter events, 0.3 us)
Async XLA Ops:
  0.6 12.5 %collective-permute-start.8 = (bf16[128,1024]{1,0:T(8,128)(2,1)}, bf16[128,1024]{1,0:T(8,128)(2,1)S(1)}, u32[]{:S(2)}, u32[]{:S(2)}) collective-permute-start(bf16[128,1024]{1,0:T(8,128)(2,1)} %refs_0_.8), channel_id=1, source_target_pairs={{0,4},{4,8},{8,12},{12,0},{1,5},{5,9},{9,13},{13,1},{2,6},{6,10},{... | collective-permute-start | bytes 786440 | tf_op jit(solution)/shard_map/ppermute | solution.py:15
  3.7 15.2 %collective-permute-start.6 = (bf16[128,1024]{1,0:T(8,128)(2,1)}, bf16[128,1024]{1,0:T(8,128)(2,1)S(1)}, u32[]{:S(2)}, u32[]{:S(2)}) collective-permute-start(bf16[128,1024]{1,0:T(8,128)(2,1)} %refs_0_.8), channel_id=1, source_target_pairs={{0,12},{4,0},{8,4},{12,8},{1,13},{5,1},{9,5},{13,9},{2,14},{6,2},{... | collective-permute-start | bytes 786440 | tf_op jit(solution)/shard_map/ppermute | solution.py:15
  5.8 14.1 %collective-permute-start.1 = (s32[8,128]{1,0:T(8,128)}, s32[8,128]{1,0:T(8,128)S(1)}, u32[]{:S(2)}, u32[]{:S(2)}) collective-permute-start(s32[8,128]{1,0:T(8,128)} %bitcast.73), channel_id=1, source_target_pairs={{0,8},{4,12},{8,0},{12,4},{1,9},{5,13},{9,1},{13,5},{2,10},{6,14},... | collective-permute-start | bytes 12296 | tf_op jit(solution)/shard_map/ppermute | solution.py:15
  6.7 14.4 %collective-permute-start = (s32[8,128]{1,0:T(8,128)}, s32[8,128]{1,0:T(8,128)S(1)}, u32[]{:S(2)}, u32[]{:S(2)}) collective-permute-start(s32[8,128]{1,0:T(8,128)} %bitcast.74), channel_id=1, source_target_pairs={{0,12},{4,0},{8,4},{12,8},{1,13},{5,1},{9,5},{13,9},{2,14},{6,2},{... | collective-permute-start | bytes 12296 | tf_op jit(solution)/shard_map/ppermute | solution.py:15
  8.1 14.4 %collective-permute-start.2 = (s32[8,128]{1,0:T(8,128)}, s32[8,128]{1,0:T(8,128)S(1)}, u32[]{:S(2)}, u32[]{:S(2)}) collective-permute-start(s32[8,128]{1,0:T(8,128)} %bitcast.75), channel_id=1, source_target_pairs={{0,4},{4,8},{8,12},{12,0},{1,5},{5,9},{9,13},{13,1},{2,6},{6,10},{... | collective-permute-start | bytes 12296 | tf_op jit(solution)/shard_map/ppermute | solution.py:15
  13.1 12.5 %collective-permute-start.4 = (f32[8,128]{1,0:T(8,128)}, f32[8,128]{1,0:T(8,128)S(1)}, u32[]{:S(2)}, u32[]{:S(2)}) collective-permute-start(f32[8,128]{1,0:T(8,128)} %bitcast.77), channel_id=1, source_target_pairs={{0,8},{4,12},{8,0},{12,4},{1,9},{5,13},{9,1},{13,5},{2,10},{6,14},... | collective-permute-start | bytes 12296 | tf_op jit(solution)/shard_map/ppermute | solution.py:15
  19.0 6.7 %collective-permute-start.3 = (f32[8,128]{1,0:T(8,128)}, f32[8,128]{1,0:T(8,128)S(1)}, u32[]{:S(2)}, u32[]{:S(2)}) collective-permute-start(f32[8,128]{1,0:T(8,128)} %bitcast.78), channel_id=1, source_target_pairs={{0,12},{4,0},{8,4},{12,8},{1,13},{5,1},{9,5},{13,9},{2,14},{6,2},{... | collective-permute-start | bytes 12296 | tf_op jit(solution)/shard_map/ppermute | solution.py:15
  19.9 5.8 %collective-permute-start.5 = (f32[8,128]{1,0:T(8,128)}, f32[8,128]{1,0:T(8,128)S(1)}, u32[]{:S(2)}, u32[]{:S(2)}) collective-permute-start(f32[8,128]{1,0:T(8,128)} %bitcast.79), channel_id=1, source_target_pairs={{0,4},{4,8},{8,12},{12,0},{1,5},{5,9},{9,13},{13,1},{2,6},{6,10},{... | collective-permute-start | bytes 12296 | tf_op jit(solution)/shard_map/ppermute | solution.py:15
  21.1 6.9 %collective-permute-start.9 = (bf16[64,1024]{1,0:T(8,128)(2,1)S(1)}, bf16[64,1024]{1,0:T(8,128)(2,1)S(1)}, u32[]{:S(2)}, u32[]{:S(2)}) collective-permute-start(bf16[64,1024]{1,0:T(8,128)(2,1)S(1)} %slice.61), channel_id=1, source_target_pairs={{0,4},{4,8},{8,12},{12,0},{1,5},{5,9},{9,13},{13,1},{2,6},{6,10},{... | collective-permute-start | bytes 393224 | tf_op jit(solution)/shard_map/ppermute | solution.py:15
  22.5 6.4 %collective-permute-start.7 = (bf16[64,1024]{1,0:T(8,128)(2,1)S(1)}, bf16[64,1024]{1,0:T(8,128)(2,1)S(1)}, u32[]{:S(2)}, u32[]{:S(2)}) collective-permute-start(bf16[64,1024]{1,0:T(8,128)(2,1)S(1)} %slice.60), channel_id=1, source_target_pairs={{0,12},{4,0},{8,4},{12,8},{1,13},{5,1},{9,5},{13,9},{2,14},{6,2},{... | collective-permute-start | bytes 393224 | tf_op jit(solution)/shard_map/ppermute | solution.py:15
  28.9 2.8 %copy-start = (bf16[4,768,1024]{2,1,0:T(8,128)(2,1)S(1)}, bf16[4,768,1024]{2,1,0:T(8,128)(2,1)}, u32[]{:S(2)}) copy-start(bf16[4,768,1024]{2,1,0:T(8,128)(2,1)} %refs_5_.7) | copy-start | bytes 18874372
  31.7 0.9 %copy-start.1 = (bf16[128,1024]{1,0:T(8,128)(2,1)S(1)}, bf16[128,1024]{1,0:T(8,128)(2,1)}, u32[]{:S(2)}) copy-start(bf16[128,1024]{1,0:T(8,128)(2,1)} %refs_0_.8) | copy-start | bytes 786436
  32.7 2.2 %copy-start.2 = (bf16[4,128,768]{2,1,0:T(8,128)(2,1)S(1)}, bf16[4,128,768]{2,1,0:T(8,128)(2,1)}, u32[]{:S(2)}) copy-start(bf16[4,128,768]{2,1,0:T(8,128)(2,1)} %refs_0_.9) | copy-start | bytes 2359300
  34.7 8.8 %collective-permute-start.16 = (bf16[1,256,768]{2,1,0:T(8,128)(2,1)S(1)}, bf16[1,256,768]{2,1,0:T(8,128)(2,1)S(1)}, u32[]{:S(2)}, u32[]{:S(2)}) collective-permute-start(bf16[1,256,768]{2,1,0:T(8,128)(2,1)S(1)} %get-tuple-element.21), channel_id=1, source_target_pairs={{0,1},{1,0},{2,3},{3,2},{4,5},{5,4},{6,7},{7,6},{8,9},{9,8},{10,11... | collective-permute-start | bytes 1179656 | tf_op jit(solution)/shard_map/ppermute | solution.py:26
  34.8 37.8 %collective-permute-start.20 = (bf16[4,128,768]{2,1,0:T(8,128)(2,1)S(1)}, bf16[4,128,768]{2,1,0:T(8,128)(2,1)S(1)}, u32[]{:S(2)}, u32[]{:S(2)}) collective-permute-start(bf16[4,128,768]{2,1,0:T(8,128)(2,1)S(1)} %copy-done.2), channel_id=1, source_target_pairs={{0,2},{1,3},{2,0},{3,1},{4,6},{5,7},{6,4},{7,5},{8,10},{9,11},{10,... | collective-permute-start | bytes 2359304 | tf_op jit(solution)/shard_map/ppermute | solution.py:26
  38.5 5.8 %collective-permute-start.14 = (bf16[1,256,768]{2,1,0:T(8,128)(2,1)S(1)}, bf16[1,256,768]{2,1,0:T(8,128)(2,1)S(1)}, u32[]{:S(2)}, u32[]{:S(2)}) collective-permute-start(bf16[1,256,768]{2,1,0:T(8,128)(2,1)S(1)} %get-tuple-element.19), channel_id=1, source_target_pairs={{0,1},{1,0},{2,3},{3,2},{4,5},{5,4},{6,7},{7,6},{8,9},{9,8},{10,11... | collective-permute-start | bytes 1179656 | tf_op jit(solution)/shard_map/ppermute | solution.py:26
  40.8 5.1 %collective-permute-start.12 = (bf16[1,256,768]{2,1,0:T(8,128)(2,1)S(1)}, bf16[1,256,768]{2,1,0:T(8,128)(2,1)S(1)}, u32[]{:S(2)}, u32[]{:S(2)}) collective-permute-start(bf16[1,256,768]{2,1,0:T(8,128)(2,1)S(1)} %get-tuple-element.17), channel_id=1, source_target_pairs={{0,1},{1,0},{2,3},{3,2},{4,5},{5,4},{6,7},{7,6},{8,9},{9,8},{10,11... | collective-permute-start | bytes 1179656 | tf_op jit(solution)/shard_map/ppermute | solution.py:26
  43.3 3.3 %collective-permute-start.10 = (bf16[1,256,768]{2,1,0:T(8,128)(2,1)S(1)}, bf16[1,256,768]{2,1,0:T(8,128)(2,1)S(1)}, u32[]{:S(2)}, u32[]{:S(2)}) collective-permute-start(bf16[1,256,768]{2,1,0:T(8,128)(2,1)S(1)} %get-tuple-element.15), channel_id=1, source_target_pairs={{0,1},{1,0},{2,3},{3,2},{4,5},{5,4},{6,7},{7,6},{8,9},{9,8},{10,11... | collective-permute-start | bytes 1179656 | tf_op jit(solution)/shard_map/ppermute | solution.py:26
  43.6 15.8 %collective-permute-start.17 = (bf16[128,768]{1,0:T(8,128)(2,1)S(1)}, bf16[128,768]{1,0:T(8,128)(2,1)S(1)}, u32[]{:S(2)}, u32[]{:S(2)}) collective-permute-start(bf16[128,768]{1,0:T(8,128)(2,1)S(1)} %fusion.19), channel_id=1, source_target_pairs={{0,2},{1,3},{2,0},{3,1},{4,6},{5,7},{6,4},{7,5},{8,10},{9,11},{10,... | collective-permute-start | bytes 589832 | tf_op jit(solution)/shard_map/ppermute | solution.py:26
  44.3 19.3 %collective-permute-start.15 = (bf16[128,768]{1,0:T(8,128)(2,1)S(1)}, bf16[128,768]{1,0:T(8,128)(2,1)S(1)}, u32[]{:S(2)}, u32[]{:S(2)}) collective-permute-start(bf16[128,768]{1,0:T(8,128)(2,1)S(1)} %fusion.18), channel_id=1, source_target_pairs={{0,2},{1,3},{2,0},{3,1},{4,6},{5,7},{6,4},{7,5},{8,10},{9,11},{10,... | collective-permute-start | bytes 589832 | tf_op jit(solution)/shard_map/ppermute | solution.py:26
  46.0 21.9 %collective-permute-start.13 = (bf16[128,768]{1,0:T(8,128)(2,1)S(1)}, bf16[128,768]{1,0:T(8,128)(2,1)S(1)}, u32[]{:S(2)}, u32[]{:S(2)}) collective-permute-start(bf16[128,768]{1,0:T(8,128)(2,1)S(1)} %fusion.17), channel_id=1, source_target_pairs={{0,2},{1,3},{2,0},{3,1},{4,6},{5,7},{6,4},{7,5},{8,10},{9,11},{10,... | collective-permute-start | bytes 589832 | tf_op jit(solution)/shard_map/ppermute | solution.py:26
  46.7 24.9 %collective-permute-start.11 = (bf16[128,768]{1,0:T(8,128)(2,1)S(1)}, bf16[128,768]{1,0:T(8,128)(2,1)S(1)}, u32[]{:S(2)}, u32[]{:S(2)}) collective-permute-start(bf16[128,768]{1,0:T(8,128)(2,1)S(1)} %fusion.16), channel_id=1, source_target_pairs={{0,2},{1,3},{2,0},{3,1},{4,6},{5,7},{6,4},{7,5},{8,10},{9,11},{10,... | collective-permute-start | bytes 589832 | tf_op jit(solution)/shard_map/ppermute | solution.py:26
  72.0 1.2 %collective-permute-start.18 = (f32[4,768]{1,0:T(4,128)S(1)}, f32[4,768]{1,0:T(4,128)S(1)}, u32[]{:S(2)}, u32[]{:S(2)}) collective-permute-start(f32[4,768]{1,0:T(4,128)S(1)} %pad_maximum_fusion.2), channel_id=1, source_target_pairs={{0,1},{1,0},{2,3},{3,2},{4,5},{5,4},{6,7},{7,6},{8,9},{9,8},{10,11... | collective-permute-start | bytes 36872 | tf_op jit(solution)/shard_map/ppermute | solution.py:26
  72.1 5.6 %collective-permute-start.21 = (bf16[4,128,768]{2,1,0:T(8,128)(2,1)S(1)}, bf16[4,128,768]{2,1,0:T(8,128)(2,1)S(1)}, u32[]{:S(2)}, u32[]{:S(2)}) collective-permute-start(bf16[4,128,768]{2,1,0:T(8,128)(2,1)S(1)} %copy-done.2), channel_id=1, source_target_pairs={{0,1},{1,0},{2,3},{3,2},{4,5},{5,4},{6,7},{7,6},{8,9},{9,8},{10,11... | collective-permute-start | bytes 2359304 | tf_op jit(solution)/shard_map/ppermute | solution.py:26
  72.6 5.1 %collective-permute-start.22 = (bf16[4,128,768]{2,1,0:T(8,128)(2,1)S(1)}, bf16[4,128,768]{2,1,0:T(8,128)(2,1)S(1)}, u32[]{:S(2)}, u32[]{:S(2)}) collective-permute-start(bf16[4,128,768]{2,1,0:T(8,128)(2,1)S(1)} %collective-permute-done.20.refs_1_), channel_id=1, source_target_pairs={{0,1},{1,0},{2,3},{3,2},{4,5},{5,4},{6,7},{7,6},{8,9},{9,8},{10,11... | collective-permute-start | bytes 2359304 | tf_op jit(solution)/shard_map/ppermute | solution.py:26
  73.3 3.8 %collective-permute-start.19 = (f32[4,768]{1,0:T(4,128)S(1)}, f32[4,768]{1,0:T(4,128)S(1)}, u32[]{:S(2)}, u32[]{:S(2)}) collective-permute-start(f32[4,768]{1,0:T(4,128)S(1)} %fusion.23), channel_id=1, source_target_pairs={{0,2},{1,3},{2,0},{3,1},{4,6},{5,7},{6,4},{7,5},{8,10},{9,11},{10,... | collective-permute-start | bytes 36872 | tf_op jit(solution)/shard_map/ppermute | solution.py:26

commit v2 on v0

v2 whole, which is shorter than its diff:
```python
import functools

import jax
import jax.numpy as jnp
from jax import lax
from jax.experimental import pallas as pl
from jax.experimental.pallas import tpu as pltpu
from jax.sharding import PartitionSpec as P

CORES = 2
ROWS = 16
VMEM_LIMIT = 24 * 2**20
VMEM = pl.BlockSpec(memory_space=pltpu.VMEM)
HBM = pl.BlockSpec(memory_space=pltpu.HBM)


def exchange(value, step):
    count = lax.axis_size("expert")
    return lax.ppermute(value, "expert", [(i, i ^ step) for i in range(count)])


def dp_shift(value, chip_step, core_flip):
    chips = lax.axis_size("dp") // CORES
    pairs = []
    for chip in range(chips):
        for core in range(CORES):
            target = (chip - chip_step) % chips
            pairs.append((chip * CORES + core, target * CORES + (core ^ core_flip)))
    return lax.ppermute(value, "dp", pairs)


def pack(out_grad, routes, route_prob):
    tokens, columns = out_grad.shape
    assert 2 * tokens <= columns and 2 * routes.shape[1] == ROWS
    value = route_prob.T
    high = lax.reduce_precision(value, 8, 7)
    middle = lax.reduce_precision(value - high, 8, 7)
    upper = jnp.concatenate([routes.T.astype(jnp.float32), high], axis=1)
    lower = jnp.concatenate([middle, value - high - middle], axis=1)
    known = jnp.concatenate([upper, lower], axis=0).astype(jnp.bfloat16)
    known = jnp.pad(known, ((0, 0), (0, columns - known.shape[1])))
    return jnp.concatenate([out_grad, known], axis=0)


def saved_at(block, chips):
    index = lax.axis_index("dp")
    chip, core = index // CORES, index % CORES
    return (block % CORES != core) * chips + (block // CORES - chip + chips) % chips


def phase_body(group, parts, *refs):
    blocks, weight = refs[:group], refs[group]
    routed, keep, send, made = refs[-4:]
    experts, rows, columns = routed.shape
    chips = keep.shape[0]
    capacity, share = rows // group, rows // parts
    tokens, fanout = blocks[0].shape[0] - ROWS, ROWS // 2
    mine, index = lax.axis_index("expert"), lax.axis_index("dp")
    chip, core = index // CORES, index % CORES

    before = (
        lax.broadcasted_iota(jnp.int32, (tokens, tokens), 0)
        < lax.broadcasted_iota(jnp.int32, (tokens, tokens), 1)
    )
    before = before.astype(jnp.float32).astype(jnp.bfloat16)
    slots = lax.broadcasted_iota(jnp.int32, (capacity, tokens), 0)
    for g in range(group):
        known = blocks[g][tokens:, : 2 * tokens].astype(jnp.float32)
        names = known[:fanout, :tokens]
        probs = known[:fanout, tokens:] + known[fanout:, :tokens] + known[fanout:, tokens:]
        named, weights = [], []
        for e in range(experts):
            hit = names == (mine * experts + e).astype(jnp.float32)
            prob = jnp.where(hit, probs, 0.0)
            named.append(jnp.max(hit.astype(jnp.float32), axis=0, keepdims=True))
            weights.append(jnp.sum(prob, axis=0, keepdims=True))
        named = jnp.concatenate(named, axis=0)
        rank = jnp.dot(named.astype(jnp.bfloat16), before, preferred_element_type=jnp.float32)
        place = jnp.where(named > 0.0, rank, -1.0).astype(jnp.int32)
        for e in range(experts):
            taken = slots == place[e : e + 1, :]
            chosen = jnp.dot(
                taken.astype(jnp.float32).astype(jnp.bfloat16),
                blocks[g][:tokens],
                preferred_element_type=jnp.float32,
            )
            scale = jnp.sum(jnp.where(taken, weights[e], 0.0), axis=1, keepdims=True)
            routed[e, g * capacity : (g + 1) * capacity, :] = (chosen * scale).astype(jnp.bfloat16)
    for e in range(experts):
        value = lax.dot_general(
            weight[e], routed[e], (((1,), (1,)), ((), ())), preferred_element_type=jnp.float32
        )
        value = value.T.astype(jnp.bfloat16)
        for p in range(parts):
            made[e * parts + p] = value[p * share : (p + 1) * share]
    for k in range(chips):
        near = (chip + k) % chips * CORES
        keep[k] = made[near + core]
        send[k] = made[near + 1 - core]


def phase(blocks, down_weight, capacity, parts, after):
    experts, hidden, columns = down_weight.shape
    group = len(blocks)
    rows = group * capacity
    chips = experts * parts // CORES
    half = jax.ShapeDtypeStruct((chips, rows // parts, hidden), jnp.bfloat16)
    return pl.pallas_call(
        functools.partial(phase_body, group, parts),
        in_specs=[VMEM] * (group + 1) + [HBM] * len(after),
        out_specs=[VMEM] * 3,
        out_shape=[jax.ShapeDtypeStruct((experts, rows, columns), jnp.bfloat16), half, half],
        scratch_shapes=[pltpu.VMEM((experts * parts, rows // parts, hidden), jnp.bfloat16)],
        compiler_params=pltpu.CompilerParams(vmem_limit_bytes=VMEM_LIMIT),
        cost_estimate=pl.CostEstimate(
            flops=2 * experts * rows * columns * hidden,
            bytes_accessed=2 * experts * hidden * columns,
            transcendentals=0,
        ),
    )(*blocks, down_weight, *after)


def score_body(phases, pieces, group, parts, *refs):
    out, table = refs[-2:]
    spread, capacity, _ = table.shape
    saved, hidden = refs[:spread], refs[spread : spread + pieces]
    per = len(hidden) // phases
    chips = spread // CORES
    mine, index = lax.axis_index("expert"), lax.axis_index("dp")
    expert = index // parts
    row = index % parts * hidden[0].shape[0]
    for i in range(spread):
        table[i] = saved[i][expert]
    total = jnp.zeros((1, out.shape[1]), jnp.float32)
    for j in range(phases):
        grad = hidden[j * per][...]
        for more in hidden[j * per + 1 : (j + 1) * per]:
            grad = grad + more[...].astype(jnp.float32)
        at = saved_at(mine ^ (j * group + row // capacity), chips)
        offset = pl.multiple_of(row % capacity, ROWS)
        kept = table[at, pl.ds(offset, grad.shape[0]), :].astype(jnp.float32)
        total = total + jnp.sum((kept * grad) ** 2, axis=0, keepdims=True)
    line = lax.broadcasted_iota(jnp.int32, out.shape, 0)
    out[...] = jnp.where(line == expert, total, 0.0)


def score(saved, hidden, group, parts, after):
    experts, share, width = saved[0].shape
    flat = [piece for pieces in hidden for piece in pieces]
    return pl.pallas_call(
        functools.partial(score_body, len(hidden), len(flat), group, parts),
        in_specs=[VMEM] * (len(saved) + len(flat)) + [HBM] * len(after),
        out_specs=VMEM,
        out_shape=jax.ShapeDtypeStruct((experts, width), jnp.float32),
        scratch_shapes=[pltpu.VMEM((len(saved), share, width), jnp.bfloat16)],
        compiler_params=pltpu.CompilerParams(vmem_limit_bytes=VMEM_LIMIT),
    )(*saved, *flat, *after)


def gradient_body(spread, *refs):
    saved, routed = refs[:spread], refs[spread:-3]
    out, done, rows = refs[-3:]
    done[...] = jnp.zeros_like(done)
    e = pl.program_id(0)
    share = saved[0].shape[1]
    mine, index = lax.axis_index("expert"), lax.axis_index("dp")
    chips = spread // CORES
    for i in range(spread):
        near = (index // CORES + i % chips) % chips * CORES
        block = near + (index % CORES if i < chips else 1 - index % CORES)
        at = pl.multiple_of((block ^ mine) * share, share)
        rows[pl.ds(at, share), :] = saved[i][e]
    whole = jnp.concatenate([part[e] for part in routed], axis=0)
    out[0] = lax.dot_general(
        rows[...], whole, (((0,), (0,)), ((), ())), preferred_element_type=jnp.float32
    ).astype(jnp.bfloat16)


def gradient_of(saved, routed):
    experts, share, hidden = saved[0].shape
    columns = routed[0].shape[2]
    slots = share * len(saved)
    return pl.pallas_call(
        functools.partial(gradient_body, len(saved)),
        grid=(experts,),
        in_specs=[VMEM] * (len(saved) + len(routed)),
        out_specs=[
            pl.BlockSpec((1, hidden, columns), lambda e: (e, 0, 0)),
            pl.BlockSpec((8, 128), lambda e: (0, 0)),
        ],
        out_shape=[
            jax.ShapeDtypeStruct((experts, hidden, columns), jnp.bfloat16),
            jax.ShapeDtypeStruct((8, 128), jnp.float32),
        ],
        scratch_shapes=[pltpu.VMEM((slots, hidden), jnp.bfloat16)],
        compiler_params=pltpu.CompilerParams(vmem_limit_bytes=VMEM_LIMIT),
        cost_estimate=pl.CostEstimate(
            flops=2 * experts * slots * columns * hidden,
            bytes_accessed=2 * experts * hidden * columns,
            transcendentals=0,
        ),
    )(*saved, *routed)


def shards(out_grad, routes, route_prob, down_weight, saved_hidden):
    owners = lax.axis_size("expert")
    dp_count = lax.axis_size("dp")
    chips = dp_count // CORES
    experts, capacity, _ = saved_hidden.shape
    assert owners == dp_count and dp_count % experts == 0
    parts = dp_count // experts
    group = max(1, parts * ROWS // capacity)
    phases = owners // group
    index = lax.axis_index("dp")

    packed = pack(out_grad, routes, route_prob)
    blocks = [packed] + [exchange(packed, j) for j in range(1, owners)]

    saved = [saved_hidden] + [dp_shift(saved_hidden, step, 0) for step in range(1, chips)]

    order = [0, 1, 3, 2] if phases == 4 else list(range(phases))
    routed, hidden = [None] * phases, [None] * phases
    for j in order:
        routed[j], keep, send = phase(
            blocks[j * group : (j + 1) * group],
            down_weight,
            capacity,
            parts,
            [],
        )
        other = dp_shift(send, 0, 1)
        total = keep.astype(jnp.float32) + other.astype(jnp.float32)
        hidden[j] = [total[0]] + [
            dp_shift(total[step].astype(jnp.bfloat16), -step, 0) for step in range(1, chips)
        ]
    saved = saved + [dp_shift(part, 0, 1) for part in saved]
    gradient, done = gradient_of(saved, routed)
    local = score(saved, hidden, group, parts, [done])
    pieces = [
        dp_shift(local, step, flip)
        for step in range(chips)
        for flip in range(CORES)
        if step + flip
    ]
    if parts > 1:
        pieces = jnp.stack([local] + pieces).reshape(chips, CORES, experts, -1)
        pieces = jnp.where(index % CORES == 0, pieces, pieces[:, ::-1])
        scores = jnp.sum(jnp.roll(pieces, index // CORES, axis=0), axis=(0, 1))
    else:
        scores = sum(pieces, local)
    return (scores, gradient)


def solution(mesh):
    placed = (
        P(("group", "expert"), "dp"),
        P(("group", "expert"), None),
        P(("group", "expert"), None),
        P("expert", None, "dp"),
        P(("group", "expert"), "dp", None),
    )
    return jax.shard_map(
        shards,
        mesh=mesh,
        in_specs=placed,
        out_specs=(P(("group", "expert"), None), P(("group", "expert"), None, "dp")),
        check_vma=False,
    )
```

time: 197 us -> 60.5 us (0.31)
  waiting for transfers between devices: 112 us -> 22 us
  local copies, waits for them, and re-layouts: 20.5 us -> 2.99 us
  matrix products: 17 us -> 0 us
  Pallas kernels: 0 us -> 15.6 us
  between operations: 14.1 us -> 0.84 us
  other arithmetic: 15.5 us -> 3.28 us
  blocking collectives: 10.7 us -> 0 us
  starting transfers between devices: 6.54 us -> 15.4 us
    all_to_all x1 -> x0, waiting for transfers between devices: 92.5 us -> none  [shards(): lax.all_to_all(outgoing, 'expert', split_axis=1, concat_axis=1, tiled=True)]
    ppermute x0 -> x17, waiting for transfers between devices: none -> 22 us  [the longest x14 12.2 us: dp_shift(): return lax.ppermute(value, 'dp', pairs)]
    reduce_scatter x1 -> x0, waiting for transfers between devices: 19 us -> none  [shards(): lax.psum_scatter(partial_value.astype(jnp.bfloat16), 'dp', scatter_dimens...]
    dot_general x2 -> x0, matrix products: 17 us -> none  [the longest x1 9.42 us: shards(): jnp.einsum('esf,esc->efc', lax.all_gather(saved_hidden, 'dp', axis=1, til...]
    pallas_call x0 -> x6, Pallas kernels: none -> 15.6 us  [the longest x4 9.44 us: phase(): pl.pallas_call(functools.partial(phase_body, group, parts), in_specs=[VME...]
    ppermute x0 -> x17, starting transfers between devices: none -> 15.4 us  [the longest x14 9.68 us: dp_shift(): return lax.ppermute(value, 'dp', pairs)]
    psum x1 -> x0, blocking collectives: 10.7 us -> none  [shards(): scores = lax.psum(local_scores, 'dp')]
    unnamed x7 -> x6, local copies, waits for them, and re-layouts: 12.3 us -> 2.79 us
  transfers between devices with their start and end apart: 3 -> 17, of which waited for: 2 -> 9; matrix products, arithmetic and copies ran while one was open for 14% -> 1% of each run, Pallas kernels for 0% -> 25%
where the time goes in v2:
time: 60.5 us; the launch traced here: 60.1 us
  waiting for transfers between devices  22 us (36%)
  Pallas kernels  15.6 us (26%)
  starting transfers between devices  15.4 us (25%)
  other arithmetic  3.28 us (5%)
  local copies, waits for them, and re-layouts  2.99 us (5%)
  between operations  0.84 us (1%)
    ppermute x14, waiting for transfers between devices, dp_shift(): return lax.ppermute(value, 'dp', pairs)  12.2 us
    ppermute x3, waiting for transfers between devices, exchange(): return lax.ppermute(value, 'expert', [(i, i ^ step) for i in range(count)])  9.76 us
    ppermute x14, starting transfers between devices, dp_shift(): return lax.ppermute(value, 'dp', pairs)  9.68 us
    pallas_call x4, Pallas kernels, phase(): pl.pallas_call(functools.partial(phase_body, group, parts), in_specs=[VME...  9.44 us
    ppermute x3, starting transfers between devices, exchange(): return lax.ppermute(value, 'expert', [(i, i ^ step) for i in range(count)])  5.75 us
    pallas_call x1, Pallas kernels, gradient_of(): pl.pallas_call(functools.partial(gradient_body, len(saved)), grid=(expert...  5.59 us
    unnamed x6, local copies, waits for them, and re-layouts  2.79 us
  transfers between devices with their start and end apart: 17, of which 9 were waited for; matrix products, arithmetic and copies ran while one was open for 1% of the time, Pallas kernels for 25%

profile of v2, /device:TPU:0, one launch (start us, length us, event | category | flops | bytes accessed | tf_op | source)
XLA Modules:
  0.0 60.1 jit_solution(17458074879532401023)
XLA Ops:
  0.6 0.7 %fusion.12 = bf16[8,128]{1,0:T(8,128)(2,1)S(1)} fusion(s32[128,8]{0,1:T(8,128)} %param.6), kind=kLoop, calls=%fused_computation.32 | loop fusion | flops 2048 | bytes 6144 | tf_op jit(solution)/shard_map/convert_element_type | solution.py:38
  1.3 0.7 %reduce-precision_convert_fusion.1 = (bf16[8,128]{1,0:T(8,128)(2,1)S(1)}, bf16[8,128]{1,0:T(8,128)(2,1)S(1)}, bf16[8,128]{1,0:T(8,128)(2,1)S(1)}) fusion(f32[128,8]{0,1:T(8,128)} %param.7), kind=kLoop, calls=%fused_computation.29 | loop fusion | flops 7168 | bytes 10240 | tf_op jit(solution)/shard_map/convert.9
  2.0 1.0 %pad_maximum_fusion.refs_0_ = bf16[144,1024]{1,0:T(8,128)(2,1)S(1)} fusion(bf16[16,1024]{1,0:T(8,128)(2,1)S(1)} %fusion.9, bf16[128,1024]{1,0:T(8,128)(2,1)} %param.5), kind=kLoop, calls=%fused_computation.12 | loop fusion | flops 589824 | bytes 589824 | tf_op jit(solution)/shard_map/concatenate | solution.py:42
  3.0 3.1 %collective-permute-start.5 = (bf16[144,1024]{1,0:T(8,128)(2,1)S(1)}, bf16[144,1024]{1,0:T(8,128)(2,1)S(1)}, u32[]{:S(2)}, u32[]{:S(2)}) collective-permute-start(bf16[144,1024]{1,0:T(8,128)(2,1)S(1)} %pad_maximum_fusion.refs_0_), channel_id=1, source_target_pairs={{0,4},{4,0},{8,12},{12,8},{1,5},{5,1},{9,13},{13,9},{2,6},{6,2},{1... | collective-permute-start | bytes 884744 | tf_op jit(solution)/shard_map/ppermute | solution.py:19
  6.1 2.6 %collective-permute-start.8 = (bf16[144,1024]{1,0:T(8,128)(2,1)S(1)}, bf16[144,1024]{1,0:T(8,128)(2,1)S(1)}, u32[]{:S(2)}, u32[]{:S(2)}) collective-permute-start(bf16[144,1024]{1,0:T(8,128)(2,1)S(1)} %pad_maximum_fusion.refs_0_), channel_id=1, source_target_pairs={{0,8},{4,12},{8,0},{12,4},{1,9},{5,13},{9,1},{13,5},{2,10},{6,14},... | collective-permute-start | bytes 884744 | tf_op jit(solution)/shard_map/ppermute | solution.py:19
  8.7 2.8 %copy-done = bf16[4,768,1024]{2,1,0:T(8,128)(2,1)S(1)} copy-done((bf16[4,768,1024]{2,1,0:T(8,128)(2,1)S(1)}, bf16[4,768,1024]{2,1,0:T(8,128)(2,1)}, u32[]{:S(2)}) %copy-start) | copy-done | bytes 6291480
  11.5 2.4 %shard_map.68 = (bf16[4,128,1024]{2,1,0:T(8,128)(2,1)S(1)}, bf16[2,128,768]{2,1,0:T(8,128)(2,1)S(1)}, bf16[2,128,768]{2,1,0:T(8,128)(2,1)S(1)}) custom-call(bf16[144,1024]{1,0:T(8,128)(2,1)S(1)} %pad_maximum_fusion.refs_0_, bf16[4,768,1024]{2,1,0:T(8,128)(2,1)S(1)} %copy-done), custom_call_target="tpu_custom_call" | custom-call | flops 805306368 | bytes 6291456 | tf_op jit(solution)/shard_map/pallas_call | solution.py:108
  13.8 0.1 collective-permute-start.3
  13.9 0.1 collective-permute-start.11
  14.0 0.4 collective-permute-start.1
  14.4 4.9 %collective-permute-done.5.refs_0_ = bf16[144,1024]{1,0:T(8,128)(2,1)S(1)} collective-permute-done((bf16[144,1024]{1,0:T(8,128)(2,1)S(1)}, bf16[144,1024]{1,0:T(8,128)(2,1)S(1)}, u32[]{:S(2)}, u32[]{:S(2)}) %collective-permute-start.5) | collective-permute-done | bytes 294944 | tf_op jit(solution)/shard_map/ppermute | solution.py:19
  19.3 1.7 %collective-permute-start = (bf16[4,128,768]{2,1,0:T(8,128)(2,1)}, bf16[4,128,768]{2,1,0:T(8,128)(2,1)S(1)}, u32[]{:S(2)}, u32[]{:S(2)}) collective-permute-start(bf16[4,128,768]{2,1,0:T(8,128)(2,1)} %refs_0_.3), channel_id=1, source_target_pairs={{0,2},{1,3},{2,0},{3,1},{4,6},{5,7},{6,4},{7,5},{8,10},{9,11},{10,... | collective-permute-start | bytes 2359304 | tf_op jit(solution)/shard_map/ppermute | solution.py:29
  21.0 2.4 %shard_map.69 = (bf16[4,128,1024]{2,1,0:T(8,128)(2,1)S(1)}, bf16[2,128,768]{2,1,0:T(8,128)(2,1)S(1)}, bf16[2,128,768]{2,1,0:T(8,128)(2,1)S(1)}) custom-call(bf16[144,1024]{1,0:T(8,128)(2,1)S(1)} %collective-permute-done.5.refs_0_, bf16[4,768,1024]{2,1,0:T(8,128)(2,1)S(1)} %copy-done.1), custom_call_target="tpu_custom_call" | custom-call | flops 805306368 | bytes 6291456 | tf_op jit(solution)/shard_map/pallas_call | solution.py:108
  23.3 4.9 %collective-permute-done.8.refs_0_ = bf16[144,1024]{1,0:T(8,128)(2,1)S(1)} collective-permute-done((bf16[144,1024]{1,0:T(8,128)(2,1)S(1)}, bf16[144,1024]{1,0:T(8,128)(2,1)S(1)}, u32[]{:S(2)}, u32[]{:S(2)}) %collective-permute-start.8) | collective-permute-done | bytes 294944 | tf_op jit(solution)/shard_map/ppermute | solution.py:19
  28.2 0.0 collective-permute-start.6
  28.2 2.4 %shard_map.70 = (bf16[4,128,1024]{2,1,0:T(8,128)(2,1)S(1)}, bf16[2,128,768]{2,1,0:T(8,128)(2,1)S(1)}, bf16[2,128,768]{2,1,0:T(8,128)(2,1)S(1)}) custom-call(bf16[144,1024]{1,0:T(8,128)(2,1)S(1)} %collective-permute-done.8.refs_0_, bf16[4,768,1024]{2,1,0:T(8,128)(2,1)S(1)} %copy-done.1), custom_call_target="tpu_custom_call" | custom-call | flops 805306368 | bytes 6291456 | tf_op jit(solution)/shard_map/pallas_call | solution.py:108
  30.6 0.0 collective-permute-done.11.refs_0_
  30.6 0.6 collective-permute-start.9
  31.1 2.4 %shard_map.71 = (bf16[4,128,1024]{2,1,0:T(8,128)(2,1)S(1)}, bf16[2,128,768]{2,1,0:T(8,128)(2,1)S(1)}, bf16[2,128,768]{2,1,0:T(8,128)(2,1)S(1)}) custom-call(bf16[144,1024]{1,0:T(8,128)(2,1)S(1)} %collective-permute-done.11.refs_0_, bf16[4,768,1024]{2,1,0:T(8,128)(2,1)S(1)} %copy-done.1), custom_call_target="tpu_custom_call" | custom-call | flops 805306368 | bytes 6291456 | tf_op jit(solution)/shard_map/pallas_call | solution.py:108
  33.5 0.0 copy-start.2
  33.5 0.0 collective-permute-done.3
  33.5 0.1 collective-permute-start.12
  33.6 0.1 convert_add_fusion.3
  33.8 1.5 %collective-permute-start.4 = (bf16[128,768]{1,0:T(8,128)(2,1)S(1)}, bf16[128,768]{1,0:T(8,128)(2,1)S(1)}, u32[]{:S(2)}, u32[]{:S(2)}) collective-permute-start(bf16[128,768]{1,0:T(8,128)(2,1)S(1)} %fusion), channel_id=1, source_target_pairs={{0,2},{1,3},{2,0},{3,1},{4,6},{5,7},{6,4},{7,5},{8,10},{9,11},{10,... | collective-permute-start | bytes 589832 | tf_op jit(solution)/shard_map/ppermute | solution.py:29
  35.3 0.1 convert_add_fusion.2
  35.4 0.0 collective-permute-done.9
  35.5 0.6 %collective-permute-start.7 = (bf16[128,768]{1,0:T(8,128)(2,1)S(1)}, bf16[128,768]{1,0:T(8,128)(2,1)S(1)}, u32[]{:S(2)}, u32[]{:S(2)}) collective-permute-start(bf16[128,768]{1,0:T(8,128)(2,1)S(1)} %fusion.1), channel_id=1, source_target_pairs={{0,2},{1,3},{2,0},{3,1},{4,6},{5,7},{6,4},{7,5},{8,10},{9,11},{10,... | collective-permute-start | bytes 589832 | tf_op jit(solution)/shard_map/ppermute | solution.py:29
  36.1 0.1 convert_add_fusion.1
  36.2 0.0 collective-permute-done.12
  36.2 1.5 %collective-permute-start.10 = (bf16[128,768]{1,0:T(8,128)(2,1)S(1)}, bf16[128,768]{1,0:T(8,128)(2,1)S(1)}, u32[]{:S(2)}, u32[]{:S(2)}) collective-permute-start(bf16[128,768]{1,0:T(8,128)(2,1)S(1)} %fusion.2), channel_id=1, source_target_pairs={{0,2},{1,3},{2,0},{3,1},{4,6},{5,7},{6,4},{7,5},{8,10},{9,11},{10,... | collective-permute-start | bytes 589832 | tf_op jit(solution)/shard_map/ppermute | solution.py:29
  37.7 0.1 convert_add_fusion
  37.8 1.7 %collective-permute-done.refs_1_ = bf16[4,128,768]{2,1,0:T(8,128)(2,1)S(1)} collective-permute-done((bf16[4,128,768]{2,1,0:T(8,128)(2,1)}, bf16[4,128,768]{2,1,0:T(8,128)(2,1)S(1)}, u32[]{:S(2)}, u32[]{:S(2)}) %collective-permute-start) | collective-permute-done | bytes 786464 | tf_op jit(solution)/shard_map/ppermute | solution.py:29
  39.5 0.0 collective-permute-start.2
  39.6 0.0 collective-permute-done.1.refs_2_
  39.6 1.3 %collective-permute-start.13 = (bf16[128,768]{1,0:T(8,128)(2,1)S(1)}, bf16[128,768]{1,0:T(8,128)(2,1)S(1)}, u32[]{:S(2)}, u32[]{:S(2)}) collective-permute-start(bf16[128,768]{1,0:T(8,128)(2,1)S(1)} %fusion.3), channel_id=1, source_target_pairs={{0,2},{1,3},{2,0},{3,1},{4,6},{5,7},{6,4},{7,5},{8,10},{9,11},{10,... | collective-permute-start | bytes 589832 | tf_op jit(solution)/shard_map/ppermute | solution.py:29
  40.9 0.9 %collective-permute-done.2.refs_3_ = bf16[4,128,768]{2,1,0:T(8,128)(2,1)S(1)} collective-permute-done((bf16[4,128,768]{2,1,0:T(8,128)(2,1)S(1)}, bf16[4,128,768]{2,1,0:T(8,128)(2,1)S(1)}, u32[]{:S(2)}, u32[]{:S(2)}) %collective-permute-start.2) | collective-permute-done | bytes 786464 | tf_op jit(solution)/shard_map/ppermute | solution.py:29
  41.8 5.6 %shard_map.72 = (bf16[4,768,1024]{2,1,0:T(8,128)(2,1)}, f32[8,128]{1,0:T(8,128)S(1)}) custom-call(bf16[4,128,768]{2,1,0:T(8,128)(2,1)S(1)} %copy-done.2, bf16[4,128,768]{2,1,0:T(8,128)(2,1)S(1)} %collective-permute-done.refs_1_, bf16[4,128,768]{2,1,0:T(8,128)(2,1)S(1)} %collective-permute-done.1.refs_2_, ...), custom_call_target="tpu_custom_call" | custom-call | flops 3221225472 | bytes 6291456 | tf_op jit(solution)/shard_map/pallas_call | solution.py:183
  47.4 0.5 collective-permute-done.7.refs_7_
  47.9 4.2 %collective-permute-done.10.refs_9_ = bf16[128,768]{1,0:T(8,128)(2,1)S(1)} collective-permute-done((bf16[128,768]{1,0:T(8,128)(2,1)S(1)}, bf16[128,768]{1,0:T(8,128)(2,1)S(1)}, u32[]{:S(2)}, u32[]{:S(2)}) %collective-permute-start.10) | collective-permute-done | bytes 196640 | tf_op jit(solution)/shard_map/ppermute | solution.py:29
  52.1 3.0 %collective-permute-done.13.refs_11_ = bf16[128,768]{1,0:T(8,128)(2,1)S(1)} collective-permute-done((bf16[128,768]{1,0:T(8,128)(2,1)S(1)}, bf16[128,768]{1,0:T(8,128)(2,1)S(1)}, u32[]{:S(2)}, u32[]{:S(2)}) %collective-permute-start.13) | collective-permute-done | bytes 196640 | tf_op jit(solution)/shard_map/ppermute | solution.py:29
  55.1 0.5 shard_map.73
  55.6 0.1 collective-permute-start.16
  55.7 1.4 %collective-permute-start.15 = (f32[4,768]{1,0:T(4,128)S(1)}, f32[4,768]{1,0:T(4,128)S(1)}, u32[]{:S(2)}, u32[]{:S(2)}) collective-permute-start(f32[4,768]{1,0:T(4,128)S(1)} %shard_map.73), channel_id=1, source_target_pairs={{0,2},{1,3},{2,0},{3,1},{4,6},{5,7},{6,4},{7,5},{8,10},{9,11},{10,... | collective-permute-start | bytes 36872 | tf_op jit(solution)/shard_map/ppermute | solution.py:29
  57.1 0.4 collective-permute-start.14
  57.5 1.3 %collective-permute-done.16 = f32[4,768]{1,0:T(4,128)S(1)} collective-permute-done((f32[4,768]{1,0:T(4,128)S(1)}, f32[4,768]{1,0:T(4,128)S(1)}, u32[]{:S(2)}, u32[]{:S(2)}) %collective-permute-start.16) | collective-permute-done | bytes 12320 | tf_op jit(solution)/shard_map/ppermute | solution.py:29
  58.8 0.6 %collective-permute-done.15 = f32[4,768]{1,0:T(4,128)S(1)} collective-permute-done((f32[4,768]{1,0:T(4,128)S(1)}, f32[4,768]{1,0:T(4,128)S(1)}, u32[]{:S(2)}, u32[]{:S(2)}) %collective-permute-start.15) | collective-permute-done | bytes 12320 | tf_op jit(solution)/shard_map/ppermute | solution.py:29
  59.5 0.0 collective-permute-done.14
  59.5 0.6 %add_add_fusion = f32[4,768]{1,0:T(4,128)} fusion(f32[4,768]{1,0:T(4,128)S(1)} %collective-permute-done.16, f32[4,768]{1,0:T(4,128)S(1)} %collective-permute-done.15, f32[4,768]{1,0:T(4,128)S(1)} %shard_map.73, f32[4,768]{1,0:T(4,128)S(1)} %collective-permute-done.14), kind=kLoop, calls=%fused_computation.25 | loop fusion | flops 9216 | bytes 61440 | tf_op jit(solution)/shard_map/add | solution.py:250
  (15 shorter events, 0.2 us)
Async XLA Ops:
  3.0 16.3 %collective-permute-start.5 = (bf16[144,1024]{1,0:T(8,128)(2,1)S(1)}, bf16[144,1024]{1,0:T(8,128)(2,1)S(1)}, u32[]{:S(2)}, u32[]{:S(2)}) collective-permute-start(bf16[144,1024]{1,0:T(8,128)(2,1)S(1)} %pad_maximum_fusion.refs_0_), channel_id=1, source_target_pairs={{0,4},{4,0},{8,12},{12,8},{1,5},{5,1},{9,13},{13,9},{2,6},{6,2},{1... | collective-permute-start | bytes 884744 | tf_op jit(solution)/shard_map/ppermute | solution.py:19
  6.1 22.1 %collective-permute-start.8 = (bf16[144,1024]{1,0:T(8,128)(2,1)S(1)}, bf16[144,1024]{1,0:T(8,128)(2,1)S(1)}, u32[]{:S(2)}, u32[]{:S(2)}) collective-permute-start(bf16[144,1024]{1,0:T(8,128)(2,1)S(1)} %pad_maximum_fusion.refs_0_), channel_id=1, source_target_pairs={{0,8},{4,12},{8,0},{12,4},{1,9},{5,13},{9,1},{13,5},{2,10},{6,14},... | collective-permute-start | bytes 884744 | tf_op jit(solution)/shard_map/ppermute | solution.py:19
  8.7 2.8 %copy-start = (bf16[4,768,1024]{2,1,0:T(8,128)(2,1)S(1)}, bf16[4,768,1024]{2,1,0:T(8,128)(2,1)}, u32[]{:S(2)}) copy-start(bf16[4,768,1024]{2,1,0:T(8,128)(2,1)} %refs_1_.7) | copy-start | bytes 18874372
  11.5 9.5 %copy-start.1 = (bf16[4,768,1024]{2,1,0:T(8,128)(2,1)S(1)}, bf16[4,768,1024]{2,1,0:T(8,128)(2,1)}, u32[]{:S(2)}) copy-start(bf16[4,768,1024]{2,1,0:T(8,128)(2,1)} %refs_1_.7) | copy-start | bytes 18874372
  13.8 19.7 %collective-permute-start.3 = (bf16[2,128,768]{2,1,0:T(8,128)(2,1)S(1)}, bf16[2,128,768]{2,1,0:T(8,128)(2,1)S(1)}, u32[]{:S(2)}, u32[]{:S(2)}) collective-permute-start(bf16[2,128,768]{2,1,0:T(8,128)(2,1)S(1)} %get-tuple-element.17), channel_id=1, source_target_pairs={{0,1},{1,0},{2,3},{3,2},{4,5},{5,4},{6,7},{7,6},{8,9},{9,8},{10,11... | collective-permute-start | bytes 1179656 | tf_op jit(solution)/shard_map/ppermute | solution.py:29
  13.9 16.7 %collective-permute-start.11 = (bf16[144,1024]{1,0:T(8,128)(2,1)S(1)}, bf16[144,1024]{1,0:T(8,128)(2,1)S(1)}, u32[]{:S(2)}, u32[]{:S(2)}) collective-permute-start(bf16[144,1024]{1,0:T(8,128)(2,1)S(1)} %pad_maximum_fusion.refs_0_), channel_id=1, source_target_pairs={{0,12},{4,8},{8,4},{12,0},{1,13},{5,9},{9,5},{13,1},{2,14},{6,10},... | collective-permute-start | bytes 884744 | tf_op jit(solution)/shard_map/ppermute | solution.py:19
  14.0 25.6 %collective-permute-start.1 = (bf16[4,128,768]{2,1,0:T(8,128)(2,1)}, bf16[4,128,768]{2,1,0:T(8,128)(2,1)S(1)}, u32[]{:S(2)}, u32[]{:S(2)}) collective-permute-start(bf16[4,128,768]{2,1,0:T(8,128)(2,1)} %refs_0_.3), channel_id=1, source_target_pairs={{0,1},{1,0},{2,3},{3,2},{4,5},{5,4},{6,7},{7,6},{8,9},{9,8},{10,11... | collective-permute-start | bytes 2359304 | tf_op jit(solution)/shard_map/ppermute | solution.py:29
  19.3 20.2 %collective-permute-start = (bf16[4,128,768]{2,1,0:T(8,128)(2,1)}, bf16[4,128,768]{2,1,0:T(8,128)(2,1)S(1)}, u32[]{:S(2)}, u32[]{:S(2)}) collective-permute-start(bf16[4,128,768]{2,1,0:T(8,128)(2,1)} %refs_0_.3), channel_id=1, source_target_pairs={{0,2},{1,3},{2,0},{3,1},{4,6},{5,7},{6,4},{7,5},{8,10},{9,11},{10,... | collective-permute-start | bytes 2359304 | tf_op jit(solution)/shard_map/ppermute | solution.py:29
  28.2 5.6 %collective-permute-start.6 = (bf16[2,128,768]{2,1,0:T(8,128)(2,1)S(1)}, bf16[2,128,768]{2,1,0:T(8,128)(2,1)S(1)}, u32[]{:S(2)}, u32[]{:S(2)}) collective-permute-start(bf16[2,128,768]{2,1,0:T(8,128)(2,1)S(1)} %get-tuple-element.19), channel_id=1, source_target_pairs={{0,1},{1,0},{2,3},{3,2},{4,5},{5,4},{6,7},{7,6},{8,9},{9,8},{10,11... | collective-permute-start | bytes 1179656 | tf_op jit(solution)/shard_map/ppermute | solution.py:29
  30.6 4.9 %collective-permute-start.9 = (bf16[2,128,768]{2,1,0:T(8,128)(2,1)S(1)}, bf16[2,128,768]{2,1,0:T(8,128)(2,1)S(1)}, u32[]{:S(2)}, u32[]{:S(2)}) collective-permute-start(bf16[2,128,768]{2,1,0:T(8,128)(2,1)S(1)} %get-tuple-element.21), channel_id=1, source_target_pairs={{0,1},{1,0},{2,3},{3,2},{4,5},{5,4},{6,7},{7,6},{8,9},{9,8},{10,11... | collective-permute-start | bytes 1179656 | tf_op jit(solution)/shard_map/ppermute | solution.py:29
  33.5 8.2 %copy-start.2 = (bf16[4,128,768]{2,1,0:T(8,128)(2,1)S(1)}, bf16[4,128,768]{2,1,0:T(8,128)(2,1)}, u32[]{:S(2)}) copy-start(bf16[4,128,768]{2,1,0:T(8,128)(2,1)} %refs_0_.3) | copy-start | bytes 2359300
  33.5 2.6 %collective-permute-start.12 = (bf16[2,128,768]{2,1,0:T(8,128)(2,1)S(1)}, bf16[2,128,768]{2,1,0:T(8,128)(2,1)S(1)}, u32[]{:S(2)}, u32[]{:S(2)}) collective-permute-start(bf16[2,128,768]{2,1,0:T(8,128)(2,1)S(1)} %get-tuple-element.23), channel_id=1, source_target_pairs={{0,1},{1,0},{2,3},{3,2},{4,5},{5,4},{6,7},{7,6},{8,9},{9,8},{10,11... | collective-permute-start | bytes 1179656 | tf_op jit(solution)/shard_map/ppermute | solution.py:29
  33.8 13.6 %collective-permute-start.4 = (bf16[128,768]{1,0:T(8,128)(2,1)S(1)}, bf16[128,768]{1,0:T(8,128)(2,1)S(1)}, u32[]{:S(2)}, u32[]{:S(2)}) collective-permute-start(bf16[128,768]{1,0:T(8,128)(2,1)S(1)} %fusion), channel_id=1, source_target_pairs={{0,2},{1,3},{2,0},{3,1},{4,6},{5,7},{6,4},{7,5},{8,10},{9,11},{10,... | collective-permute-start | bytes 589832 | tf_op jit(solution)/shard_map/ppermute | solution.py:29
  35.5 12.4 %collective-permute-start.7 = (bf16[128,768]{1,0:T(8,128)(2,1)S(1)}, bf16[128,768]{1,0:T(8,128)(2,1)S(1)}, u32[]{:S(2)}, u32[]{:S(2)}) collective-permute-start(bf16[128,768]{1,0:T(8,128)(2,1)S(1)} %fusion.1), channel_id=1, source_target_pairs={{0,2},{1,3},{2,0},{3,1},{4,6},{5,7},{6,4},{7,5},{8,10},{9,11},{10,... | collective-permute-start | bytes 589832 | tf_op jit(solution)/shard_map/ppermute | solution.py:29
  36.2 15.9 %collective-permute-start.10 = (bf16[128,768]{1,0:T(8,128)(2,1)S(1)}, bf16[128,768]{1,0:T(8,128)(2,1)S(1)}, u32[]{:S(2)}, u32[]{:S(2)}) collective-permute-start(bf16[128,768]{1,0:T(8,128)(2,1)S(1)} %fusion.2), channel_id=1, source_target_pairs={{0,2},{1,3},{2,0},{3,1},{4,6},{5,7},{6,4},{7,5},{8,10},{9,11},{10,... | collective-permute-start | bytes 589832 | tf_op jit(solution)/shard_map/ppermute | solution.py:29
  39.5 2.3 %collective-permute-start.2 = (bf16[4,128,768]{2,1,0:T(8,128)(2,1)S(1)}, bf16[4,128,768]{2,1,0:T(8,128)(2,1)S(1)}, u32[]{:S(2)}, u32[]{:S(2)}) collective-permute-start(bf16[4,128,768]{2,1,0:T(8,128)(2,1)S(1)} %collective-permute-done.refs_1_), channel_id=1, source_target_pairs={{0,1},{1,0},{2,3},{3,2},{4,5},{5,4},{6,7},{7,6},{8,9},{9,8},{10,11... | collective-permute-start | bytes 2359304 | tf_op jit(solution)/shard_map/ppermute | solution.py:29
  39.6 15.5 %collective-permute-start.13 = (bf16[128,768]{1,0:T(8,128)(2,1)S(1)}, bf16[128,768]{1,0:T(8,128)(2,1)S(1)}, u32[]{:S(2)}, u32[]{:S(2)}) collective-permute-start(bf16[128,768]{1,0:T(8,128)(2,1)S(1)} %fusion.3), channel_id=1, source_target_pairs={{0,2},{1,3},{2,0},{3,1},{4,6},{5,7},{6,4},{7,5},{8,10},{9,11},{10,... | collective-permute-start | bytes 589832 | tf_op jit(solution)/shard_map/ppermute | solution.py:29
  55.6 3.2 %collective-permute-start.16 = (f32[4,768]{1,0:T(4,128)S(1)}, f32[4,768]{1,0:T(4,128)S(1)}, u32[]{:S(2)}, u32[]{:S(2)}) collective-permute-start(f32[4,768]{1,0:T(4,128)S(1)} %shard_map.73), channel_id=1, source_target_pairs={{0,3},{1,2},{2,1},{3,0},{4,7},{5,6},{6,5},{7,4},{8,11},{9,10},{10,... | collective-permute-start | bytes 36872 | tf_op jit(solution)/shard_map/ppermute | solution.py:29
  55.7 3.8 %collective-permute-start.15 = (f32[4,768]{1,0:T(4,128)S(1)}, f32[4,768]{1,0:T(4,128)S(1)}, u32[]{:S(2)}, u32[]{:S(2)}) collective-permute-start(f32[4,768]{1,0:T(4,128)S(1)} %shard_map.73), channel_id=1, source_target_pairs={{0,2},{1,3},{2,0},{3,1},{4,6},{5,7},{6,4},{7,5},{8,10},{9,11},{10,... | collective-permute-start | bytes 36872 | tf_op jit(solution)/shard_map/ppermute | solution.py:29
  57.1 2.4 %collective-permute-start.14 = (f32[4,768]{1,0:T(4,128)S(1)}, f32[4,768]{1,0:T(4,128)S(1)}, u32[]{:S(2)}, u32[]{:S(2)}) collective-permute-start(f32[4,768]{1,0:T(4,128)S(1)} %shard_map.73), channel_id=1, source_target_pairs={{0,1},{1,0},{2,3},{3,2},{4,5},{5,4},{6,7},{7,6},{8,9},{9,8},{10,11... | collective-permute-start | bytes 36872 | tf_op jit(solution)/shard_map/ppermute | solution.py:29

commit v3 on v2

--- a/solution.py
+++ b/solution.py
@@ -9,14 +9,42 @@
 
 CORES = 2
 ROWS = 16
-VMEM_LIMIT = 24 * 2**20
+VMEM_LIMIT = 14 * 2**20
 VMEM = pl.BlockSpec(memory_space=pltpu.VMEM)
-HBM = pl.BlockSpec(memory_space=pltpu.HBM)
+ANY = pl.BlockSpec(memory_space=pl.ANY)
 
 
 def exchange(value, step):
     count = lax.axis_size("expert")
     return lax.ppermute(value, "expert", [(i, i ^ step) for i in range(count)])
+
+
+def look_up(table, index):
+    return sum(jnp.where(index == i, int(value), 0) for i, value in enumerate(table))
+
+
+def gather_plan(packed):
+    owners = lax.axis_size("expert")
+    mine = lax.axis_index("expert")
+    own = ([packed], [0] * owners, list(range(owners)))
+    if owners != 4:
+        return [own] + [
+            ([exchange(packed, j)], [0] * owners, [i ^ j for i in range(owners)])
+            for j in range(1, owners)
+        ]
+    send = lambda value, pairs: lax.ppermute(value, "expert", pairs)
+    down = send(packed, [(1, 0), (2, 1), (3, 2)])
+    up = send(packed, [(0, 1), (1, 2), (2, 3)])
+    far = send(packed, [(0, 2), (3, 1)])
+    outer = [(1, 0), (2, 3)]
+    second = send(jnp.where(mine == 1, down, up), outer)
+    third = send(far, outer)
+    return [
+        own,
+        ([down, up], [0, 0, 0, 1], [1, 2, 3, 2]),
+        ([second, up], [0, 1, 1, 0], [2, 0, 1, 1]),
+        ([third, far], [0, 1, 1, 0], [3, 3, 0, 0]),
+    ]
 
 
 def dp_shift(value, chip_step, core_flip):
@@ -48,13 +76,14 @@
     return (block % CORES != core) * chips + (block // CORES - chip + chips) % chips
 
 
-def phase_body(group, parts, *refs):
-    blocks, weight = refs[:group], refs[group]
-    routed, keep, send, made = refs[-4:]
+def phase_body(picks, arrays, parts, *refs):
+    group = len(picks)
+    choices, weight = refs[: sum(arrays)], refs[sum(arrays)]
+    routed, keep, send, made, table = refs[-5:]
     experts, rows, columns = routed.shape
     chips = keep.shape[0]
     capacity, share = rows // group, rows // parts
-    tokens, fanout = blocks[0].shape[0] - ROWS, ROWS // 2
+    tokens, fanout = choices[0].shape[0] - ROWS, ROWS // 2
     mine, index = lax.axis_index("expert"), lax.axis_index("dp")
     chip, core = index // CORES, index % CORES
 
@@ -64,6 +93,21 @@
     )
     before = before.astype(jnp.float32).astype(jnp.bfloat16)
     slots = lax.broadcasted_iota(jnp.int32, (capacity, tokens), 0)
+    blocks, at = [], 0
+    for g in range(group):
+        options = choices[at : at + arrays[g]]
+        at += arrays[g]
+        if len(options) == 1:
+            blocks.append(options[0])
+            continue
+        pick = look_up(picks[g], mine)
+        for i, option in enumerate(options):
+
+            @pl.when(pick == i)
+            def _(option=option, g=g):
+                table[g] = option[...]
+
+        blocks.append(table.at[g])
     for g in range(group):
         known = blocks[g][tokens:, : 2 * tokens].astype(jnp.float32)
         names = known[:fanout, :tokens]
@@ -102,29 +146,35 @@
 def phase(blocks, down_weight, capacity, parts, after):
     experts, hidden, columns = down_weight.shape
     group = len(blocks)
+    arrays = [len(options) for options, _, _ in blocks]
+    flat = [array for options, _, _ in blocks for array in options]
     rows = group * capacity
     chips = experts * parts // CORES
     half = jax.ShapeDtypeStruct((chips, rows // parts, hidden), jnp.bfloat16)
     return pl.pallas_call(
-        functools.partial(phase_body, group, parts),
-        in_specs=[VMEM] * (group + 1) + [HBM] * len(after),
+        functools.partial(phase_body, [pick for _, pick, _ in blocks], arrays, parts),
+        in_specs=[VMEM] * (len(flat) + 1) + [ANY] * len(after),
         out_specs=[VMEM] * 3,
         out_shape=[jax.ShapeDtypeStruct((experts, rows, columns), jnp.bfloat16), half, half],
-        scratch_shapes=[pltpu.VMEM((experts * parts, rows // parts, hidden), jnp.bfloat16)],
+        scratch_shapes=[
+            pltpu.VMEM((experts * parts, rows // parts, hidden), jnp.bfloat16),
+            pltpu.VMEM((group,) + flat[0].shape, jnp.bfloat16),
+        ],
         compiler_params=pltpu.CompilerParams(vmem_limit_bytes=VMEM_LIMIT),
         cost_estimate=pl.CostEstimate(
-            flops=2 * experts * rows * columns * hidden,
-            bytes_accessed=2 * experts * hidden * columns,
+            flops=5 * experts * rows * columns * hidden,
+            bytes_accessed=5 * experts * hidden * columns,
             transcendentals=0,
         ),
-    )(*blocks, down_weight, *after)
-
-
-def score_body(phases, pieces, group, parts, *refs):
+    )(*flat, down_weight, *after)
+
+
+def score_body(tables, pieces, parts, *refs):
     out, table = refs[-2:]
     spread, capacity, _ = table.shape
     saved, hidden = refs[:spread], refs[spread : spread + pieces]
-    per = len(hidden) // phases
+    phases = pieces * CORES // spread
+    group, per = len(tables) // phases, spread // CORES
     chips = spread // CORES
     mine, index = lax.axis_index("expert"), lax.axis_index("dp")
     expert = index // parts
@@ -136,7 +186,11 @@
         grad = hidden[j * per][...]
         for more in hidden[j * per + 1 : (j + 1) * per]:
             grad = grad + more[...].astype(jnp.float32)
-        at = saved_at(mine ^ (j * group + row // capacity), chips)
+        block = sum(
+            jnp.where(row // capacity == g, look_up(tables[j * group + g], mine), 0)
+            for g in range(group)
+        )
+        at = saved_at(block, chips)
         offset = pl.multiple_of(row % capacity, ROWS)
         kept = table[at, pl.ds(offset, grad.shape[0]), :].astype(jnp.float32)
         total = total + jnp.sum((kept * grad) ** 2, axis=0, keepdims=True)
@@ -144,12 +198,12 @@
     out[...] = jnp.where(line == expert, total, 0.0)
 
 
-def score(saved, hidden, group, parts, after):
+def score(saved, hidden, tables, parts, after):
     experts, share, width = saved[0].shape
     flat = [piece for pieces in hidden for piece in pieces]
     return pl.pallas_call(
-        functools.partial(score_body, len(hidden), len(flat), group, parts),
-        in_specs=[VMEM] * (len(saved) + len(flat)) + [HBM] * len(after),
+        functools.partial(score_body, tables, len(flat), parts),
+        in_specs=[VMEM] * (len(saved) + len(flat)) + [ANY] * len(after),
         out_specs=VMEM,
         out_shape=jax.ShapeDtypeStruct((experts, width), jnp.float32),
         scratch_shapes=[pltpu.VMEM((len(saved), share, width), jnp.bfloat16)],
@@ -157,7 +211,7 @@
     )(*saved, *flat, *after)
 
 
-def gradient_body(spread, *refs):
+def gradient_body(spread, tables, *refs):
     saved, routed = refs[:spread], refs[spread:-3]
     out, done, rows = refs[-3:]
     done[...] = jnp.zeros_like(done)
@@ -168,7 +222,10 @@
     for i in range(spread):
         near = (index // CORES + i % chips) % chips * CORES
         block = near + (index % CORES if i < chips else 1 - index % CORES)
-        at = pl.multiple_of((block ^ mine) * share, share)
+        order = sum(
+            jnp.where(look_up(table, mine) == block, j, 0) for j, table in enumerate(tables)
+        )
+        at = pl.multiple_of(order * share, share)
         rows[pl.ds(at, share), :] = saved[i][e]
     whole = jnp.concatenate([part[e] for part in routed], axis=0)
     out[0] = lax.dot_general(
@@ -176,12 +233,12 @@
     ).astype(jnp.bfloat16)
 
 
-def gradient_of(saved, routed):
+def gradient_of(saved, routed, tables):
     experts, share, hidden = saved[0].shape
     columns = routed[0].shape[2]
     slots = share * len(saved)
     return pl.pallas_call(
-        functools.partial(gradient_body, len(saved)),
+        functools.partial(gradient_body, len(saved), tables),
         grid=(experts,),
         in_specs=[VMEM] * (len(saved) + len(routed)),
         out_specs=[
@@ -195,8 +252,8 @@
         scratch_shapes=[pltpu.VMEM((slots, hidden), jnp.bfloat16)],
         compiler_params=pltpu.CompilerParams(vmem_limit_bytes=VMEM_LIMIT),
         cost_estimate=pl.CostEstimate(
-            flops=2 * experts * slots * columns * hidden,
-            bytes_accessed=2 * experts * hidden * columns,
+            flops=5 * experts * slots * columns * hidden,
+            bytes_accessed=5 * experts * hidden * columns,
             transcendentals=0,
         ),
     )(*saved, *routed)
@@ -214,19 +271,19 @@
     index = lax.axis_index("dp")
 
     packed = pack(out_grad, routes, route_prob)
-    blocks = [packed] + [exchange(packed, j) for j in range(1, owners)]
+    plan = gather_plan(packed)
+    tables = [table for _, _, table in plan]
 
     saved = [saved_hidden] + [dp_shift(saved_hidden, step, 0) for step in range(1, chips)]
 
-    order = [0, 1, 3, 2] if phases == 4 else list(range(phases))
     routed, hidden = [None] * phases, [None] * phases
-    for j in order:
+    for j in range(phases):
         routed[j], keep, send = phase(
-            blocks[j * group : (j + 1) * group],
+            plan[j * group : (j + 1) * group],
             down_weight,
             capacity,
             parts,
-            [],
+            hidden[0][:1] if j == 2 else hidden[0][1:] + hidden[1][:1] if j == 3 else [],
         )
         other = dp_shift(send, 0, 1)
         total = keep.astype(jnp.float32) + other.astype(jnp.float32)
@@ -234,8 +291,8 @@
             dp_shift(total[step].astype(jnp.bfloat16), -step, 0) for step in range(1, chips)
         ]
     saved = saved + [dp_shift(part, 0, 1) for part in saved]
-    gradient, done = gradient_of(saved, routed)
-    local = score(saved, hidden, group, parts, [done])
+    gradient, done = gradient_of(saved, routed, tables)
+    local = score(saved, hidden, tables, parts, [done])
     pieces = [
         dp_shift(local, step, flip)
         for step in range(chips)

time: 60.5 us -> 59.8 us (0.988)
  waiting for transfers between devices: 22 us -> 13.6 us
  starting transfers between devices: 15.4 us -> 22.9 us
    ppermute x3 -> x5, starting transfers between devices: 5.75 us -> 14.4 us  [gather_plan(): send = lambda value, pairs: lax.ppermute(value, 'expert', pairs)]
    ppermute x14, waiting for transfers between devices: 12.2 us -> 4.89 us  [dp_shift(): return lax.ppermute(value, 'dp', pairs)]
    ppermute x14, starting transfers between devices: 9.68 us -> 8.48 us  [dp_shift(): return lax.ppermute(value, 'dp', pairs)]
    ppermute x3 -> x5, waiting for transfers between devices: 9.76 us -> 8.7 us  [gather_plan(): send = lambda value, pairs: lax.ppermute(value, 'expert', pairs)]
  transfers between devices with their start and end apart: 17 -> 19, of which waited for: 9 -> 5; matrix products, arithmetic and copies ran while one was open for 1% -> 1% of each run, Pallas kernels for 25% -> 26%
where the time goes in v3:
time: 59.8 us; the launch traced here: 59.4 us
  starting transfers between devices  22.9 us (38%)
  Pallas kernels  15.8 us (26%)
  waiting for transfers between devices  13.6 us (23%)
  other arithmetic  3.32 us (6%)
  local copies, waits for them, and re-layouts  2.99 us (5%)
  between operations  0.91 us (2%)
    ppermute x5, starting transfers between devices, gather_plan(): send = lambda value, pairs: lax.ppermute(value, 'expert', pairs)  14.4 us
    pallas_call x4, Pallas kernels, phase(): pl.pallas_call(functools.partial(phase_body, [pick for _, pick, _ in bloc...  9.56 us
    ppermute x5, waiting for transfers between devices, gather_plan(): send = lambda value, pairs: lax.ppermute(value, 'expert', pairs)  8.7 us
    ppermute x14, starting transfers between devices, dp_shift(): return lax.ppermute(value, 'dp', pairs)  8.48 us
    pallas_call x1, Pallas kernels, gradient_of(): pl.pallas_call(functools.partial(gradient_body, len(saved), tables), grid...  5.68 us
    ppermute x14, waiting for transfers between devices, dp_shift(): return lax.ppermute(value, 'dp', pairs)  4.89 us
    unnamed x6, local copies, waits for them, and re-layouts  2.79 us
  transfers between devices with their start and end apart: 19, of which 5 were waited for; matrix products, arithmetic and copies ran while one was open for 1% of the time, Pallas kernels for 26%

profile of v3, /device:TPU:0, one launch (start us, length us, event | category | flops | bytes accessed | tf_op | source)
XLA Modules:
  0.0 59.4 jit_solution(1039753303752275644)
XLA Ops:
  0.6 0.7 %fusion.12 = bf16[8,128]{1,0:T(8,128)(2,1)S(1)} fusion(s32[128,8]{0,1:T(8,128)} %param.6), kind=kLoop, calls=%fused_computation.33 | loop fusion | flops 2048 | bytes 6144 | tf_op jit(solution)/shard_map/convert_element_type | solution.py:66
  1.3 0.7 %reduce-precision_convert_fusion.1 = (bf16[8,128]{1,0:T(8,128)(2,1)S(1)}, bf16[8,128]{1,0:T(8,128)(2,1)S(1)}, bf16[8,128]{1,0:T(8,128)(2,1)S(1)}) fusion(f32[128,8]{0,1:T(8,128)} %param.7), kind=kLoop, calls=%fused_computation.30 | loop fusion | flops 7168 | bytes 10240 | tf_op jit(solution)/shard_map/convert.9
  2.0 1.0 %pad_maximum_fusion.refs_0_ = bf16[144,1024]{1,0:T(8,128)(2,1)S(1)} fusion(bf16[16,1024]{1,0:T(8,128)(2,1)S(1)} %fusion.9, bf16[128,1024]{1,0:T(8,128)(2,1)} %param.5), kind=kLoop, calls=%fused_computation.12 | loop fusion | flops 589824 | bytes 589824 | tf_op jit(solution)/shard_map/concatenate | solution.py:70
  3.0 4.9 %collective-permute-start.6 = (bf16[144,1024]{1,0:T(8,128)(2,1)S(1)}, bf16[144,1024]{1,0:T(8,128)(2,1)S(1)}, u32[]{:S(2)}, u32[]{:S(2)}) collective-permute-start(bf16[144,1024]{1,0:T(8,128)(2,1)S(1)} %pad_maximum_fusion.refs_0_), channel_id=1, source_target_pairs={{0,4},{4,8},{8,12},{1,5},{5,9},{9,13},{2,6},{6,10},{10,14},{3,7},{... | collective-permute-start | bytes 884744 | tf_op jit(solution)/shard_map/ppermute | solution.py:35
  7.9 1.3 %collective-permute-start.5 = (bf16[144,1024]{1,0:T(8,128)(2,1)S(1)}, bf16[144,1024]{1,0:T(8,128)(2,1)S(1)}, u32[]{:S(2)}, u32[]{:S(2)}) collective-permute-start(bf16[144,1024]{1,0:T(8,128)(2,1)S(1)} %pad_maximum_fusion.refs_0_), channel_id=1, source_target_pairs={{4,0},{8,4},{12,8},{5,1},{9,5},{13,9},{6,2},{10,6},{14,10},{7,3},{... | collective-permute-start | bytes 884744 | tf_op jit(solution)/shard_map/ppermute | solution.py:35
  9.2 5.6 %collective-permute-start.12 = (bf16[144,1024]{1,0:T(8,128)(2,1)S(1)}, bf16[144,1024]{1,0:T(8,128)(2,1)S(1)}, u32[]{:S(2)}, u32[]{:S(2)}) collective-permute-start(bf16[144,1024]{1,0:T(8,128)(2,1)S(1)} %pad_maximum_fusion.refs_0_), channel_id=1, source_target_pairs={{0,8},{12,4},{1,9},{13,5},{2,10},{14,6},{3,11},{15,7},{16,24},{28,... | collective-permute-start | bytes 884744 | tf_op jit(solution)/shard_map/ppermute | solution.py:35
  14.8 0.1 collective-permute-start.1
  14.9 1.6 %collective-permute-start = (bf16[4,128,768]{2,1,0:T(8,128)(2,1)}, bf16[4,128,768]{2,1,0:T(8,128)(2,1)S(1)}, u32[]{:S(2)}, u32[]{:S(2)}) collective-permute-start(bf16[4,128,768]{2,1,0:T(8,128)(2,1)} %refs_0_.3), channel_id=1, source_target_pairs={{0,2},{1,3},{2,0},{3,1},{4,6},{5,7},{6,4},{7,5},{8,10},{9,11},{10,... | collective-permute-start | bytes 2359304 | tf_op jit(solution)/shard_map/ppermute | solution.py:57
  16.5 2.8 %copy-done = bf16[4,768,1024]{2,1,0:T(8,128)(2,1)S(1)} copy-done((bf16[4,768,1024]{2,1,0:T(8,128)(2,1)S(1)}, bf16[4,768,1024]{2,1,0:T(8,128)(2,1)}, u32[]{:S(2)}) %copy-start) | copy-done | bytes 6291480
  19.2 2.4 %shard_map.68 = (bf16[4,128,1024]{2,1,0:T(8,128)(2,1)S(1)}, bf16[2,128,768]{2,1,0:T(8,128)(2,1)S(1)}, bf16[2,128,768]{2,1,0:T(8,128)(2,1)S(1)}) custom-call(bf16[144,1024]{1,0:T(8,128)(2,1)S(1)} %pad_maximum_fusion.refs_0_, bf16[4,768,1024]{2,1,0:T(8,128)(2,1)S(1)} %copy-done), custom_call_target="tpu_custom_call" | custom-call | flops 2013265920 | bytes 15728640 | tf_op jit(solution)/shard_map/pallas_call | solution.py:154
  21.6 0.0 collective-permute-done.6.refs_1_
  21.6 0.2 collective-permute-start.3
  21.9 1.3 %collective-permute-start.9 = (bf16[144,1024]{1,0:T(8,128)(2,1)S(1)}, bf16[144,1024]{1,0:T(8,128)(2,1)S(1)}, u32[]{:S(2)}, u32[]{:S(2)}) collective-permute-start(bf16[144,1024]{1,0:T(8,128)(2,1)S(1)} %broadcast_select_fusion), channel_id=1, source_target_pairs={{4,0},{8,12},{5,1},{9,13},{6,2},{10,14},{7,3},{11,15},{20,16},{24,... | collective-permute-start | bytes 884744 | tf_op jit(solution)/shard_map/ppermute | solution.py:35
  23.2 2.4 %shard_map.69 = (bf16[4,128,1024]{2,1,0:T(8,128)(2,1)S(1)}, bf16[2,128,768]{2,1,0:T(8,128)(2,1)S(1)}, bf16[2,128,768]{2,1,0:T(8,128)(2,1)S(1)}) custom-call(bf16[144,1024]{1,0:T(8,128)(2,1)S(1)} %collective-permute-done.5.refs_0_, bf16[144,1024]{1,0:T(8,128)(2,1)S(1)} %collective-permute-done.6.refs_1_, bf16[4,768,1024]{2,1,0:T(8,128)(2,1)S(1)} %copy-done.1), custom_call_target="tpu_custom_call" | custom-call | flops 2013265920 | bytes 15728640 | tf_op jit(solution)/shard_map/pallas_call | solution.py:154
  25.6 0.0 collective-permute-done.12.refs_1_
  25.6 0.4 collective-permute-start.7
  26.0 1.3 %collective-permute-start.13 = (bf16[144,1024]{1,0:T(8,128)(2,1)S(1)}, bf16[144,1024]{1,0:T(8,128)(2,1)S(1)}, u32[]{:S(2)}, u32[]{:S(2)}) collective-permute-start(bf16[144,1024]{1,0:T(8,128)(2,1)S(1)} %collective-permute-done.12.refs_1_), channel_id=1, source_target_pairs={{4,0},{8,12},{5,1},{9,13},{6,2},{10,14},{7,3},{11,15},{20,16},{24,... | collective-permute-start | bytes 884744 | tf_op jit(solution)/shard_map/ppermute | solution.py:35
  27.3 0.1 convert_add_fusion.3
  27.5 6.1 %collective-permute-done.9.refs_0_ = bf16[144,1024]{1,0:T(8,128)(2,1)S(1)} collective-permute-done((bf16[144,1024]{1,0:T(8,128)(2,1)S(1)}, bf16[144,1024]{1,0:T(8,128)(2,1)S(1)}, u32[]{:S(2)}, u32[]{:S(2)}) %collective-permute-start.9) | collective-permute-done | bytes 294944 | tf_op jit(solution)/shard_map/ppermute | solution.py:35
  33.6 0.5 collective-permute-start.4
  34.1 2.4 %shard_map.70 = (bf16[4,128,1024]{2,1,0:T(8,128)(2,1)S(1)}, bf16[2,128,768]{2,1,0:T(8,128)(2,1)S(1)}, bf16[2,128,768]{2,1,0:T(8,128)(2,1)S(1)}) custom-call(bf16[144,1024]{1,0:T(8,128)(2,1)S(1)} %collective-permute-done.9.refs_0_, bf16[144,1024]{1,0:T(8,128)(2,1)S(1)} %collective-permute-done.6.refs_1_, bf16[4,768,1024]{2,1,0:T(8,128)(2,1)S(1)} %copy-done.1, ...), custom_call_target="tpu_custom_call" | custom-call | flops 2013265920 | bytes 15728640 | tf_op jit(solution)/shard_map/pallas_call | solution.py:154
  36.6 0.0 collective-permute-done.7
  36.6 0.1 collective-permute-start.10
  36.6 0.1 convert_add_fusion.2
  36.8 0.0 copy-start.2
  36.8 2.6 %collective-permute-done.13.refs_0_ = bf16[144,1024]{1,0:T(8,128)(2,1)S(1)} collective-permute-done((bf16[144,1024]{1,0:T(8,128)(2,1)S(1)}, bf16[144,1024]{1,0:T(8,128)(2,1)S(1)}, u32[]{:S(2)}, u32[]{:S(2)}) %collective-permute-start.13) | collective-permute-done | bytes 294944 | tf_op jit(solution)/shard_map/ppermute | solution.py:35
  39.4 0.5 collective-permute-start.8
  39.9 2.4 %shard_map.71 = (bf16[4,128,1024]{2,1,0:T(8,128)(2,1)S(1)}, bf16[2,128,768]{2,1,0:T(8,128)(2,1)S(1)}, bf16[2,128,768]{2,1,0:T(8,128)(2,1)S(1)}) custom-call(bf16[144,1024]{1,0:T(8,128)(2,1)S(1)} %collective-permute-done.13.refs_0_, bf16[144,1024]{1,0:T(8,128)(2,1)S(1)} %collective-permute-done.12.refs_1_, bf16[4,768,1024]{2,1,0:T(8,128)(2,1)S(1)} %copy-done.1, ...), custom_call_target="tpu_custom_call" | custom-call | flops 2013265920 | bytes 15728640 | tf_op jit(solution)/shard_map/pallas_call | solution.py:154
  42.3 0.1 collective-permute-start.14
  42.4 0.5 collective-permute-start.2
  42.9 0.0 collective-permute-done.10
  42.9 0.1 convert_add_fusion.1
  43.0 1.5 %collective-permute-start.11 = (bf16[128,768]{1,0:T(8,128)(2,1)S(1)}, bf16[128,768]{1,0:T(8,128)(2,1)S(1)}, u32[]{:S(2)}, u32[]{:S(2)}) collective-permute-start(bf16[128,768]{1,0:T(8,128)(2,1)S(1)} %fusion.2), channel_id=1, source_target_pairs={{0,2},{1,3},{2,0},{3,1},{4,6},{5,7},{6,4},{7,5},{8,10},{9,11},{10,... | collective-permute-start | bytes 589832 | tf_op jit(solution)/shard_map/ppermute | solution.py:57
  44.6 0.0 collective-permute-done.14
  44.6 0.1 convert_add_fusion
  44.7 1.1 %collective-permute-start.15 = (bf16[128,768]{1,0:T(8,128)(2,1)S(1)}, bf16[128,768]{1,0:T(8,128)(2,1)S(1)}, u32[]{:S(2)}, u32[]{:S(2)}) collective-permute-start(bf16[128,768]{1,0:T(8,128)(2,1)S(1)} %fusion.3), channel_id=1, source_target_pairs={{0,2},{1,3},{2,0},{3,1},{4,6},{5,7},{6,4},{7,5},{8,10},{9,11},{10,... | collective-permute-start | bytes 589832 | tf_op jit(solution)/shard_map/ppermute | solution.py:57
  45.8 0.0 collective-permute-done.2.refs_3_
  45.8 5.7 %shard_map.72 = (bf16[4,768,1024]{2,1,0:T(8,128)(2,1)}, f32[8,128]{1,0:T(8,128)S(1)}) custom-call(bf16[4,128,768]{2,1,0:T(8,128)(2,1)S(1)} %copy-done.2, bf16[4,128,768]{2,1,0:T(8,128)(2,1)S(1)} %collective-permute-done.refs_1_, bf16[4,128,768]{2,1,0:T(8,128)(2,1)S(1)} %collective-permute-done.1.refs_2_, ...), custom_call_target="tpu_custom_call" | custom-call | flops 8053063680 | bytes 15728640 | tf_op jit(solution)/shard_map/pallas_call | solution.py:240
  51.5 0.0 collective-permute-done.8.refs_7_
  51.5 0.0 collective-permute-done.11.refs_9_
  51.5 2.7 %collective-permute-done.15.refs_11_ = bf16[128,768]{1,0:T(8,128)(2,1)S(1)} collective-permute-done((bf16[128,768]{1,0:T(8,128)(2,1)S(1)}, bf16[128,768]{1,0:T(8,128)(2,1)S(1)}, u32[]{:S(2)}, u32[]{:S(2)}) %collective-permute-start.15) | collective-permute-done | bytes 196640 | tf_op jit(solution)/shard_map/ppermute | solution.py:57
  54.2 0.5 shard_map.73
  54.7 0.4 collective-permute-start.18
  55.1 1.2 %collective-permute-start.17 = (f32[4,768]{1,0:T(4,128)S(1)}, f32[4,768]{1,0:T(4,128)S(1)}, u32[]{:S(2)}, u32[]{:S(2)}) collective-permute-start(f32[4,768]{1,0:T(4,128)S(1)} %shard_map.73), channel_id=1, source_target_pairs={{0,2},{1,3},{2,0},{3,1},{4,6},{5,7},{6,4},{7,5},{8,10},{9,11},{10,... | collective-permute-start | bytes 36872 | tf_op jit(solution)/shard_map/ppermute | solution.py:57
  56.4 0.3 collective-permute-start.16
  56.7 1.4 %collective-permute-done.18 = f32[4,768]{1,0:T(4,128)S(1)} collective-permute-done((f32[4,768]{1,0:T(4,128)S(1)}, f32[4,768]{1,0:T(4,128)S(1)}, u32[]{:S(2)}, u32[]{:S(2)}) %collective-permute-start.18) | collective-permute-done | bytes 12320 | tf_op jit(solution)/shard_map/ppermute | solution.py:57
  58.0 0.8 %collective-permute-done.17 = f32[4,768]{1,0:T(4,128)S(1)} collective-permute-done((f32[4,768]{1,0:T(4,128)S(1)}, f32[4,768]{1,0:T(4,128)S(1)}, u32[]{:S(2)}, u32[]{:S(2)}) %collective-permute-start.17) | collective-permute-done | bytes 12320 | tf_op jit(solution)/shard_map/ppermute | solution.py:57
  58.8 0.6 %add_add_fusion = f32[4,768]{1,0:T(4,128)} fusion(f32[4,768]{1,0:T(4,128)S(1)} %collective-permute-done.18, f32[4,768]{1,0:T(4,128)S(1)} %collective-permute-done.17, f32[4,768]{1,0:T(4,128)S(1)} %shard_map.73, f32[4,768]{1,0:T(4,128)S(1)} %collective-permute-done.16), kind=kLoop, calls=%fused_computation.26 | loop fusion | flops 9216 | bytes 61440 | tf_op jit(solution)/shard_map/add | solution.py:307
  (20 shorter events, 0.3 us)
Async XLA Ops:
  3.0 18.6 %collective-permute-start.6 = (bf16[144,1024]{1,0:T(8,128)(2,1)S(1)}, bf16[144,1024]{1,0:T(8,128)(2,1)S(1)}, u32[]{:S(2)}, u32[]{:S(2)}) collective-permute-start(bf16[144,1024]{1,0:T(8,128)(2,1)S(1)} %pad_maximum_fusion.refs_0_), channel_id=1, source_target_pairs={{0,4},{4,8},{8,12},{1,5},{5,9},{9,13},{2,6},{6,10},{10,14},{3,7},{... | collective-permute-start | bytes 884744 | tf_op jit(solution)/shard_map/ppermute | solution.py:35
  7.9 13.9 %collective-permute-start.5 = (bf16[144,1024]{1,0:T(8,128)(2,1)S(1)}, bf16[144,1024]{1,0:T(8,128)(2,1)S(1)}, u32[]{:S(2)}, u32[]{:S(2)}) collective-permute-start(bf16[144,1024]{1,0:T(8,128)(2,1)S(1)} %pad_maximum_fusion.refs_0_), channel_id=1, source_target_pairs={{4,0},{8,4},{12,8},{5,1},{9,5},{13,9},{6,2},{10,6},{14,10},{7,3},{... | collective-permute-start | bytes 884744 | tf_op jit(solution)/shard_map/ppermute | solution.py:35
  9.2 16.4 %collective-permute-start.12 = (bf16[144,1024]{1,0:T(8,128)(2,1)S(1)}, bf16[144,1024]{1,0:T(8,128)(2,1)S(1)}, u32[]{:S(2)}, u32[]{:S(2)}) collective-permute-start(bf16[144,1024]{1,0:T(8,128)(2,1)S(1)} %pad_maximum_fusion.refs_0_), channel_id=1, source_target_pairs={{0,8},{12,4},{1,9},{13,5},{2,10},{14,6},{3,11},{15,7},{16,24},{28,... | collective-permute-start | bytes 884744 | tf_op jit(solution)/shard_map/ppermute | solution.py:35
  14.8 31.0 %collective-permute-start.1 = (bf16[4,128,768]{2,1,0:T(8,128)(2,1)}, bf16[4,128,768]{2,1,0:T(8,128)(2,1)S(1)}, u32[]{:S(2)}, u32[]{:S(2)}) collective-permute-start(bf16[4,128,768]{2,1,0:T(8,128)(2,1)} %refs_0_.3), channel_id=1, source_target_pairs={{0,1},{1,0},{2,3},{3,2},{4,5},{5,4},{6,7},{7,6},{8,9},{9,8},{10,11... | collective-permute-start | bytes 2359304 | tf_op jit(solution)/shard_map/ppermute | solution.py:57
  14.9 27.5 %collective-permute-start = (bf16[4,128,768]{2,1,0:T(8,128)(2,1)}, bf16[4,128,768]{2,1,0:T(8,128)(2,1)S(1)}, u32[]{:S(2)}, u32[]{:S(2)}) collective-permute-start(bf16[4,128,768]{2,1,0:T(8,128)(2,1)} %refs_0_.3), channel_id=1, source_target_pairs={{0,2},{1,3},{2,0},{3,1},{4,6},{5,7},{6,4},{7,5},{8,10},{9,11},{10,... | collective-permute-start | bytes 2359304 | tf_op jit(solution)/shard_map/ppermute | solution.py:57
  16.5 2.8 %copy-start = (bf16[4,768,1024]{2,1,0:T(8,128)(2,1)S(1)}, bf16[4,768,1024]{2,1,0:T(8,128)(2,1)}, u32[]{:S(2)}) copy-start(bf16[4,768,1024]{2,1,0:T(8,128)(2,1)} %refs_2_.5) | copy-start | bytes 18874372
  19.2 4.0 %copy-start.1 = (bf16[4,768,1024]{2,1,0:T(8,128)(2,1)S(1)}, bf16[4,768,1024]{2,1,0:T(8,128)(2,1)}, u32[]{:S(2)}) copy-start(bf16[4,768,1024]{2,1,0:T(8,128)(2,1)} %refs_2_.5) | copy-start | bytes 18874372
  21.6 4.4 %collective-permute-start.3 = (bf16[2,128,768]{2,1,0:T(8,128)(2,1)S(1)}, bf16[2,128,768]{2,1,0:T(8,128)(2,1)S(1)}, u32[]{:S(2)}, u32[]{:S(2)}) collective-permute-start(bf16[2,128,768]{2,1,0:T(8,128)(2,1)S(1)} %get-tuple-element.17), channel_id=1, source_target_pairs={{0,1},{1,0},{2,3},{3,2},{4,5},{5,4},{6,7},{7,6},{8,9},{9,8},{10,11... | collective-permute-start | bytes 1179656 | tf_op jit(solution)/shard_map/ppermute | solution.py:57
  21.9 11.7 %collective-permute-start.9 = (bf16[144,1024]{1,0:T(8,128)(2,1)S(1)}, bf16[144,1024]{1,0:T(8,128)(2,1)S(1)}, u32[]{:S(2)}, u32[]{:S(2)}) collective-permute-start(bf16[144,1024]{1,0:T(8,128)(2,1)S(1)} %broadcast_select_fusion), channel_id=1, source_target_pairs={{4,0},{8,12},{5,1},{9,13},{6,2},{10,14},{7,3},{11,15},{20,16},{24,... | collective-permute-start | bytes 884744 | tf_op jit(solution)/shard_map/ppermute | solution.py:35
  25.6 10.9 %collective-permute-start.7 = (bf16[2,128,768]{2,1,0:T(8,128)(2,1)S(1)}, bf16[2,128,768]{2,1,0:T(8,128)(2,1)S(1)}, u32[]{:S(2)}, u32[]{:S(2)}) collective-permute-start(bf16[2,128,768]{2,1,0:T(8,128)(2,1)S(1)} %get-tuple-element.19), channel_id=1, source_target_pairs={{0,1},{1,0},{2,3},{3,2},{4,5},{5,4},{6,7},{7,6},{8,9},{9,8},{10,11... | collective-permute-start | bytes 1179656 | tf_op jit(solution)/shard_map/ppermute | solution.py:57
  26.0 13.3 %collective-permute-start.13 = (bf16[144,1024]{1,0:T(8,128)(2,1)S(1)}, bf16[144,1024]{1,0:T(8,128)(2,1)S(1)}, u32[]{:S(2)}, u32[]{:S(2)}) collective-permute-start(bf16[144,1024]{1,0:T(8,128)(2,1)S(1)} %collective-permute-done.12.refs_1_), channel_id=1, source_target_pairs={{4,0},{8,12},{5,1},{9,13},{6,2},{10,14},{7,3},{11,15},{20,16},{24,... | collective-permute-start | bytes 884744 | tf_op jit(solution)/shard_map/ppermute | solution.py:35
  33.6 6.3 %collective-permute-start.4 = (bf16[128,768]{1,0:T(8,128)(2,1)S(1)}, bf16[128,768]{1,0:T(8,128)(2,1)S(1)}, u32[]{:S(2)}, u32[]{:S(2)}) collective-permute-start(bf16[128,768]{1,0:T(8,128)(2,1)S(1)} %fusion), channel_id=1, source_target_pairs={{0,2},{1,3},{2,0},{3,1},{4,6},{5,7},{6,4},{7,5},{8,10},{9,11},{10,... | collective-permute-start | bytes 589832 | tf_op jit(solution)/shard_map/ppermute | solution.py:57
  36.6 6.3 %collective-permute-start.10 = (bf16[2,128,768]{2,1,0:T(8,128)(2,1)S(1)}, bf16[2,128,768]{2,1,0:T(8,128)(2,1)S(1)}, u32[]{:S(2)}, u32[]{:S(2)}) collective-permute-start(bf16[2,128,768]{2,1,0:T(8,128)(2,1)S(1)} %get-tuple-element.21), channel_id=1, source_target_pairs={{0,1},{1,0},{2,3},{3,2},{4,5},{5,4},{6,7},{7,6},{8,9},{9,8},{10,11... | collective-permute-start | bytes 1179656 | tf_op jit(solution)/shard_map/ppermute | solution.py:57
  36.8 9.0 %copy-start.2 = (bf16[4,128,768]{2,1,0:T(8,128)(2,1)S(1)}, bf16[4,128,768]{2,1,0:T(8,128)(2,1)}, u32[]{:S(2)}) copy-start(bf16[4,128,768]{2,1,0:T(8,128)(2,1)} %refs_0_.3) | copy-start | bytes 2359300
  39.4 12.1 %collective-permute-start.8 = (bf16[128,768]{1,0:T(8,128)(2,1)S(1)}, bf16[128,768]{1,0:T(8,128)(2,1)S(1)}, u32[]{:S(2)}, u32[]{:S(2)}) collective-permute-start(bf16[128,768]{1,0:T(8,128)(2,1)S(1)} %fusion.1), channel_id=1, source_target_pairs={{0,2},{1,3},{2,0},{3,1},{4,6},{5,7},{6,4},{7,5},{8,10},{9,11},{10,... | collective-permute-start | bytes 589832 | tf_op jit(solution)/shard_map/ppermute | solution.py:57
  42.3 2.3 %collective-permute-start.14 = (bf16[2,128,768]{2,1,0:T(8,128)(2,1)S(1)}, bf16[2,128,768]{2,1,0:T(8,128)(2,1)S(1)}, u32[]{:S(2)}, u32[]{:S(2)}) collective-permute-start(bf16[2,128,768]{2,1,0:T(8,128)(2,1)S(1)} %get-tuple-element.23), channel_id=1, source_target_pairs={{0,1},{1,0},{2,3},{3,2},{4,5},{5,4},{6,7},{7,6},{8,9},{9,8},{10,11... | collective-permute-start | bytes 1179656 | tf_op jit(solution)/shard_map/ppermute | solution.py:57
  42.4 3.4 %collective-permute-start.2 = (bf16[4,128,768]{2,1,0:T(8,128)(2,1)S(1)}, bf16[4,128,768]{2,1,0:T(8,128)(2,1)S(1)}, u32[]{:S(2)}, u32[]{:S(2)}) collective-permute-start(bf16[4,128,768]{2,1,0:T(8,128)(2,1)S(1)} %collective-permute-done.refs_1_), channel_id=1, source_target_pairs={{0,1},{1,0},{2,3},{3,2},{4,5},{5,4},{6,7},{7,6},{8,9},{9,8},{10,11... | collective-permute-start | bytes 2359304 | tf_op jit(solution)/shard_map/ppermute | solution.py:57
  43.0 8.5 %collective-permute-start.11 = (bf16[128,768]{1,0:T(8,128)(2,1)S(1)}, bf16[128,768]{1,0:T(8,128)(2,1)S(1)}, u32[]{:S(2)}, u32[]{:S(2)}) collective-permute-start(bf16[128,768]{1,0:T(8,128)(2,1)S(1)} %fusion.2), channel_id=1, source_target_pairs={{0,2},{1,3},{2,0},{3,1},{4,6},{5,7},{6,4},{7,5},{8,10},{9,11},{10,... | collective-permute-start | bytes 589832 | tf_op jit(solution)/shard_map/ppermute | solution.py:57
  44.7 9.5 %collective-permute-start.15 = (bf16[128,768]{1,0:T(8,128)(2,1)S(1)}, bf16[128,768]{1,0:T(8,128)(2,1)S(1)}, u32[]{:S(2)}, u32[]{:S(2)}) collective-permute-start(bf16[128,768]{1,0:T(8,128)(2,1)S(1)} %fusion.3), channel_id=1, source_target_pairs={{0,2},{1,3},{2,0},{3,1},{4,6},{5,7},{6,4},{7,5},{8,10},{9,11},{10,... | collective-permute-start | bytes 589832 | tf_op jit(solution)/shard_map/ppermute | solution.py:57
  54.7 3.3 %collective-permute-start.18 = (f32[4,768]{1,0:T(4,128)S(1)}, f32[4,768]{1,0:T(4,128)S(1)}, u32[]{:S(2)}, u32[]{:S(2)}) collective-permute-start(f32[4,768]{1,0:T(4,128)S(1)} %shard_map.73), channel_id=1, source_target_pairs={{0,3},{1,2},{2,1},{3,0},{4,7},{5,6},{6,5},{7,4},{8,11},{9,10},{10,... | collective-permute-start | bytes 36872 | tf_op jit(solution)/shard_map/ppermute | solution.py:57
  55.1 3.7 %collective-permute-start.17 = (f32[4,768]{1,0:T(4,128)S(1)}, f32[4,768]{1,0:T(4,128)S(1)}, u32[]{:S(2)}, u32[]{:S(2)}) collective-permute-start(f32[4,768]{1,0:T(4,128)S(1)} %shard_map.73), channel_id=1, source_target_pairs={{0,2},{1,3},{2,0},{3,1},{4,6},{5,7},{6,4},{7,5},{8,10},{9,11},{10,... | collective-permute-start | bytes 36872 | tf_op jit(solution)/shard_map/ppermute | solution.py:57
  56.4 2.5 %collective-permute-start.16 = (f32[4,768]{1,0:T(4,128)S(1)}, f32[4,768]{1,0:T(4,128)S(1)}, u32[]{:S(2)}, u32[]{:S(2)}) collective-permute-start(f32[4,768]{1,0:T(4,128)S(1)} %shard_map.73), channel_id=1, source_target_pairs={{0,1},{1,0},{2,3},{3,2},{4,5},{5,4},{6,7},{7,6},{8,9},{9,8},{10,11... | collective-permute-start | bytes 36872 | tf_op jit(solution)/shard_map/ppermute | solution.py:57

commit v4 on v3

--- a/solution.py
+++ b/solution.py
@@ -169,10 +169,23 @@
     )(*flat, down_weight, *after)
 
 
+def copy_expert(first, second, expert, target):
+    early = first.shape[0]
+
+    @pl.when(expert < early)
+    def _():
+        target[...] = first[jnp.minimum(expert, early - 1)]
+
+    @pl.when(expert >= early)
+    def _():
+        target[...] = second[jnp.maximum(expert - early, 0)]
+
+
 def score_body(tables, pieces, parts, *refs):
     out, table = refs[-2:]
     spread, capacity, _ = table.shape
-    saved, hidden = refs[:spread], refs[spread : spread + pieces]
+    first, second = refs[:spread], refs[spread : 2 * spread]
+    hidden = refs[2 * spread : 2 * spread + pieces]
     phases = pieces * CORES // spread
     group, per = len(tables) // phases, spread // CORES
     chips = spread // CORES
@@ -180,7 +193,7 @@
     expert = index // parts
     row = index % parts * hidden[0].shape[0]
     for i in range(spread):
-        table[i] = saved[i][expert]
+        copy_expert(first[i], second[i], expert, table.at[i])
     total = jnp.zeros((1, out.shape[1]), jnp.float32)
     for j in range(phases):
         grad = hidden[j * per][...]
@@ -199,24 +212,26 @@
 
 
 def score(saved, hidden, tables, parts, after):
-    experts, share, width = saved[0].shape
+    spread = len(saved) // 2
+    _, share, width = saved[0].shape
+    experts = saved[0].shape[0] + saved[spread].shape[0]
     flat = [piece for pieces in hidden for piece in pieces]
     return pl.pallas_call(
         functools.partial(score_body, tables, len(flat), parts),
         in_specs=[VMEM] * (len(saved) + len(flat)) + [ANY] * len(after),
         out_specs=VMEM,
         out_shape=jax.ShapeDtypeStruct((experts, width), jnp.float32),
-        scratch_shapes=[pltpu.VMEM((len(saved), share, width), jnp.bfloat16)],
+        scratch_shapes=[pltpu.VMEM((spread, share, width), jnp.bfloat16)],
         compiler_params=pltpu.CompilerParams(vmem_limit_bytes=VMEM_LIMIT),
     )(*saved, *flat, *after)
 
 
 def gradient_body(spread, tables, *refs):
-    saved, routed = refs[:spread], refs[spread:-3]
+    first, second, routed = refs[:spread], refs[spread : 2 * spread], refs[2 * spread : -3]
     out, done, rows = refs[-3:]
     done[...] = jnp.zeros_like(done)
     e = pl.program_id(0)
-    share = saved[0].shape[1]
+    share = first[0].shape[1]
     mine, index = lax.axis_index("expert"), lax.axis_index("dp")
     chips = spread // CORES
     for i in range(spread):
@@ -226,7 +241,7 @@
             jnp.where(look_up(table, mine) == block, j, 0) for j, table in enumerate(tables)
         )
         at = pl.multiple_of(order * share, share)
-        rows[pl.ds(at, share), :] = saved[i][e]
+        copy_expert(first[i], second[i], e, rows.at[pl.ds(at, share)])
     whole = jnp.concatenate([part[e] for part in routed], axis=0)
     out[0] = lax.dot_general(
         rows[...], whole, (((0,), (0,)), ((), ())), preferred_element_type=jnp.float32
@@ -234,11 +249,12 @@
 
 
 def gradient_of(saved, routed, tables):
-    experts, share, hidden = saved[0].shape
-    columns = routed[0].shape[2]
-    slots = share * len(saved)
+    spread = len(saved) // 2
+    _, share, hidden = saved[0].shape
+    experts, _, columns = routed[0].shape
+    slots = share * spread
     return pl.pallas_call(
-        functools.partial(gradient_body, len(saved), tables),
+        functools.partial(gradient_body, spread, tables),
         grid=(experts,),
         in_specs=[VMEM] * (len(saved) + len(routed)),
         out_specs=[
@@ -274,7 +290,10 @@
     plan = gather_plan(packed)
     tables = [table for _, _, table in plan]
 
-    saved = [saved_hidden] + [dp_shift(saved_hidden, step, 0) for step in range(1, chips)]
+    halves = [saved_hidden[: experts // 2], saved_hidden[experts // 2 :]]
+    halves = [
+        [half] + [dp_shift(half, step, 0) for step in range(1, chips)] for half in halves
+    ]
 
     routed, hidden = [None] * phases, [None] * phases
     for j in range(phases):
@@ -283,14 +302,21 @@
             down_weight,
             capacity,
             parts,
-            hidden[0][:1] if j == 2 else hidden[0][1:] + hidden[1][:1] if j == 3 else [],
+            halves[0][1:]
+            if j == 0
+            else hidden[0][:1]
+            if j == 2
+            else hidden[0][1:] + hidden[1][:1]
+            if j == 3
+            else [],
         )
         other = dp_shift(send, 0, 1)
         total = keep.astype(jnp.float32) + other.astype(jnp.float32)
         hidden[j] = [total[0]] + [
             dp_shift(total[step].astype(jnp.bfloat16), -step, 0) for step in range(1, chips)
         ]
-    saved = saved + [dp_shift(part, 0, 1) for part in saved]
+    halves = [half + [dp_shift(part, 0, 1) for part in half] for half in halves]
+    saved = halves[0] + halves[1]
     gradient, done = gradient_of(saved, routed, tables)
     local = score(saved, hidden, tables, parts, [done])
     pieces = [

time: 59.8 us -> 90.4 us (1.51)
  waiting for transfers between devices: 13.6 us -> 40.8 us
  starting transfers between devices: 22.9 us -> 25.1 us
  local copies, waits for them, and re-layouts: 2.99 us -> 4.16 us
    ppermute x14 -> x17, waiting for transfers between devices: 4.89 us -> 26.6 us  [dp_shift(): return lax.ppermute(value, 'dp', pairs)]
    ppermute x5, waiting for transfers between devices: 8.7 us -> 14.2 us  [gather_plan(): send = lambda value, pairs: lax.ppermute(value, 'expert', pairs)]
    ppermute x14 -> x17, starting transfers between devices: 8.48 us -> 10.7 us  [dp_shift(): return lax.ppermute(value, 'dp', pairs)]
    slice x0 -> x1, local copies, waits for them, and re-layouts: none -> 1.17 us  [shards(): halves = [saved_hidden[:experts // 2], saved_hidden[experts // 2:]]]
    unnamed x6 -> x4, local copies, waits for them, and re-layouts: 2.79 us -> 2.79 us
  transfers between devices with their start and end apart: 19 -> 22, of which waited for: 5 -> 8; matrix products, arithmetic and copies ran while one was open for 1% -> 2% of each run, Pallas kernels for 26% -> 17%
where the time goes in v4:
time: 90.4 us; the launch traced here: 90 us
  waiting for transfers between devices  40.8 us (45%)
  starting transfers between devices  25.1 us (28%)
  Pallas kernels  15.7 us (17%)
  local copies, waits for them, and re-layouts  4.16 us (5%)
  other arithmetic  3.32 us (4%)
    ppermute x17, waiting for transfers between devices, dp_shift(): return lax.ppermute(value, 'dp', pairs)  26.6 us
    ppermute x5, starting transfers between devices, gather_plan(): send = lambda value, pairs: lax.ppermute(value, 'expert', pairs)  14.4 us
    ppermute x5, waiting for transfers between devices, gather_plan(): send = lambda value, pairs: lax.ppermute(value, 'expert', pairs)  14.2 us
    ppermute x17, starting transfers between devices, dp_shift(): return lax.ppermute(value, 'dp', pairs)  10.7 us
    pallas_call x4, Pallas kernels, phase(): pl.pallas_call(functools.partial(phase_body, [pick for _, pick, _ in bloc...  9.55 us
    pallas_call x1, Pallas kernels, gradient_of(): pl.pallas_call(functools.partial(gradient_body, spread, tables), grid=(ex...  5.76 us
    unnamed x4, local copies, waits for them, and re-layouts  2.79 us
  transfers between devices with their start and end apart: 22, of which 8 were waited for; matrix products, arithmetic and copies ran while one was open for 2% of the time, Pallas kernels for 17%

profile of v4, /device:TPU:0, one launch (start us, length us, event | category | flops | bytes accessed | tf_op | source)
XLA Modules:
  0.0 90.0 jit_solution(16398351574595723439)
XLA Ops:
  0.6 0.7 fusion.12
  1.3 0.7 reduce-precision_convert_fusion.1
  2.0 1.0 %pad_maximum_fusion.refs_0_ = bf16[144,1024]{1,0:T(8,128)(2,1)S(1)} fusion(bf16[16,1024]{1,0:T(8,128)(2,1)S(1)} %fusion.9, bf16[128,1024]{1,0:T(8,128)(2,1)} %param.5), kind=kLoop, calls=%fused_computation.12 | loop fusion | flops 589824 | bytes 589824 | tf_op jit(solution)/shard_map/concatenate | solution.py:70
  3.0 4.9 %collective-permute-start.9 = (bf16[144,1024]{1,0:T(8,128)(2,1)S(1)}, bf16[144,1024]{1,0:T(8,128)(2,1)S(1)}, u32[]{:S(2)}, u32[]{:S(2)}) collective-permute-start(bf16[144,1024]{1,0:T(8,128)(2,1)S(1)} %pad_maximum_fusion.refs_0_), channel_id=1, source_target_pairs={{0,4},{4,8},{8,12},{1,5},{5,9},{9,13},{2,6},{6,10},{10,14},{3,7},{... | collective-permute-start | bytes 884744 | tf_op jit(solution)/shard_map/ppermute | solution.py:35
  7.9 1.3 %collective-permute-start.8 = (bf16[144,1024]{1,0:T(8,128)(2,1)S(1)}, bf16[144,1024]{1,0:T(8,128)(2,1)S(1)}, u32[]{:S(2)}, u32[]{:S(2)}) collective-permute-start(bf16[144,1024]{1,0:T(8,128)(2,1)S(1)} %pad_maximum_fusion.refs_0_), channel_id=1, source_target_pairs={{4,0},{8,4},{12,8},{5,1},{9,5},{13,9},{6,2},{10,6},{14,10},{7,3},{... | collective-permute-start | bytes 884744 | tf_op jit(solution)/shard_map/ppermute | solution.py:35
  9.2 5.6 %collective-permute-start.15 = (bf16[144,1024]{1,0:T(8,128)(2,1)S(1)}, bf16[144,1024]{1,0:T(8,128)(2,1)S(1)}, u32[]{:S(2)}, u32[]{:S(2)}) collective-permute-start(bf16[144,1024]{1,0:T(8,128)(2,1)S(1)} %pad_maximum_fusion.refs_0_), channel_id=1, source_target_pairs={{0,8},{12,4},{1,9},{13,5},{2,10},{14,6},{3,11},{15,7},{16,24},{28,... | collective-permute-start | bytes 884744 | tf_op jit(solution)/shard_map/ppermute | solution.py:35
  14.8 1.2 %fusion.13 = (bf16[2,128,768]{2,1,0:T(8,128)(2,1)S(1)}, bf16[2,128,768]{2,1,0:T(8,128)(2,1)S(1)}) fusion(bf16[4,128,768]{2,1,0:T(8,128)(2,1)} %param.9), kind=kLoop, calls=%fused_computation.34 | loop fusion | bytes 1572864 | tf_op jit(solution)/shard_map/slice | solution.py:293
  16.0 0.1 collective-permute-start.4
  16.1 1.6 %collective-permute-start.3 = (bf16[2,128,768]{2,1,0:T(8,128)(2,1)S(1)}, bf16[2,128,768]{2,1,0:T(8,128)(2,1)S(1)}, u32[]{:S(2)}, u32[]{:S(2)}) collective-permute-start(bf16[2,128,768]{2,1,0:T(8,128)(2,1)S(1)} %get-tuple-element.30.refs_4_), channel_id=1, source_target_pairs={{0,2},{1,3},{2,0},{3,1},{4,6},{5,7},{6,4},{7,5},{8,10},{9,11},{10,... | collective-permute-start | bytes 1179656 | tf_op jit(solution)/shard_map/ppermute | solution.py:57
  17.6 0.5 collective-permute-start
  18.2 0.1 collective-permute-done.8.refs_0_
  18.3 2.8 %copy-done = bf16[4,768,1024]{2,1,0:T(8,128)(2,1)S(1)} copy-done((bf16[4,768,1024]{2,1,0:T(8,128)(2,1)S(1)}, bf16[4,768,1024]{2,1,0:T(8,128)(2,1)}, u32[]{:S(2)}) %copy-start) | copy-done | bytes 6291480
  21.1 2.4 %shard_map.69 = (bf16[4,128,1024]{2,1,0:T(8,128)(2,1)S(1)}, bf16[2,128,768]{2,1,0:T(8,128)(2,1)S(1)}, bf16[2,128,768]{2,1,0:T(8,128)(2,1)S(1)}) custom-call(bf16[144,1024]{1,0:T(8,128)(2,1)S(1)} %collective-permute-done.8.refs_0_, bf16[144,1024]{1,0:T(8,128)(2,1)S(1)} %collective-permute-done.9.refs_1_, bf16[4,768,1024]{2,1,0:T(8,128)(2,1)S(1)} %copy-done), custom_call_target="tpu_custom_call" | custom-call | flops 2013265920 | bytes 15728640 | tf_op jit(solution)/shard_map/pallas_call | solution.py:154
  23.5 0.1 collective-permute-start.10
  23.6 12.4 %collective-permute-done.refs_2_.refs_1_ = bf16[2,128,768]{2,1,0:T(8,128)(2,1)S(1)} collective-permute-done((bf16[2,128,768]{2,1,0:T(8,128)(2,1)S(1)}, bf16[2,128,768]{2,1,0:T(8,128)(2,1)S(1)}, u32[]{:S(2)}, u32[]{:S(2)}) %collective-permute-start) | collective-permute-done | bytes 393248 | tf_op jit(solution)/shard_map/ppermute | solution.py:57
  36.0 0.0 collective-permute-start.1
  36.0 2.4 %shard_map.68 = (bf16[4,128,1024]{2,1,0:T(8,128)(2,1)S(1)}, bf16[2,128,768]{2,1,0:T(8,128)(2,1)S(1)}, bf16[2,128,768]{2,1,0:T(8,128)(2,1)S(1)}) custom-call(bf16[144,1024]{1,0:T(8,128)(2,1)S(1)} %pad_maximum_fusion.refs_0_, bf16[4,768,1024]{2,1,0:T(8,128)(2,1)S(1)} %copy-done.1, bf16[2,128,768]{2,1,0:T(8,128)(2,1)S(1)} %collective-permute-done.refs_2_.refs_1_), custom_call_target="tpu_custom_call" | custom-call | flops 2013265920 | bytes 15728640 | tf_op jit(solution)/shard_map/pallas_call | solution.py:154
  38.4 0.6 collective-permute-start.6
  39.0 0.1 convert_add_fusion.2
  39.1 0.0 collective-permute-done.15.refs_1_
  39.1 1.3 %collective-permute-start.12 = (bf16[144,1024]{1,0:T(8,128)(2,1)S(1)}, bf16[144,1024]{1,0:T(8,128)(2,1)S(1)}, u32[]{:S(2)}, u32[]{:S(2)}) collective-permute-start(bf16[144,1024]{1,0:T(8,128)(2,1)S(1)} %broadcast_select_fusion), channel_id=1, source_target_pairs={{4,0},{8,12},{5,1},{9,13},{6,2},{10,14},{7,3},{11,15},{20,16},{24,... | collective-permute-start | bytes 884744 | tf_op jit(solution)/shard_map/ppermute | solution.py:35
  40.5 1.3 %collective-permute-start.16 = (bf16[144,1024]{1,0:T(8,128)(2,1)S(1)}, bf16[144,1024]{1,0:T(8,128)(2,1)S(1)}, u32[]{:S(2)}, u32[]{:S(2)}) collective-permute-start(bf16[144,1024]{1,0:T(8,128)(2,1)S(1)} %collective-permute-done.15.refs_1_), channel_id=1, source_target_pairs={{4,0},{8,12},{5,1},{9,13},{6,2},{10,14},{7,3},{11,15},{20,16},{24,... | collective-permute-start | bytes 884744 | tf_op jit(solution)/shard_map/ppermute | solution.py:35
  41.8 0.1 convert_add_fusion.3
  41.9 0.0 collective-permute-done.3.refs_5_
  41.9 0.3 collective-permute-start.2
  42.2 14.1 %collective-permute-done.16.refs_0_ = bf16[144,1024]{1,0:T(8,128)(2,1)S(1)} collective-permute-done((bf16[144,1024]{1,0:T(8,128)(2,1)S(1)}, bf16[144,1024]{1,0:T(8,128)(2,1)S(1)}, u32[]{:S(2)}, u32[]{:S(2)}) %collective-permute-start.16) | collective-permute-done | bytes 294944 | tf_op jit(solution)/shard_map/ppermute | solution.py:35
  56.3 1.5 %collective-permute-start.7 = (bf16[128,768]{1,0:T(8,128)(2,1)S(1)}, bf16[128,768]{1,0:T(8,128)(2,1)S(1)}, u32[]{:S(2)}, u32[]{:S(2)}) collective-permute-start(bf16[128,768]{1,0:T(8,128)(2,1)S(1)} %fusion), channel_id=1, source_target_pairs={{0,2},{1,3},{2,0},{3,1},{4,6},{5,7},{6,4},{7,5},{8,10},{9,11},{10,... | collective-permute-start | bytes 589832 | tf_op jit(solution)/shard_map/ppermute | solution.py:57
  57.8 2.4 %shard_map.70 = (bf16[4,128,1024]{2,1,0:T(8,128)(2,1)S(1)}, bf16[2,128,768]{2,1,0:T(8,128)(2,1)S(1)}, bf16[2,128,768]{2,1,0:T(8,128)(2,1)S(1)}) custom-call(bf16[144,1024]{1,0:T(8,128)(2,1)S(1)} %collective-permute-done.12.refs_0_, bf16[144,1024]{1,0:T(8,128)(2,1)S(1)} %collective-permute-done.9.refs_1_, bf16[4,768,1024]{2,1,0:T(8,128)(2,1)S(1)} %copy-done.1, ...), custom_call_target="tpu_custom_call" | custom-call | flops 2013265920 | bytes 15728640 | tf_op jit(solution)/shard_map/pallas_call | solution.py:154
  60.2 3.4 %collective-permute-done.7.refs_3_.refs_9_ = bf16[128,768]{1,0:T(8,128)(2,1)S(1)} collective-permute-done((bf16[128,768]{1,0:T(8,128)(2,1)S(1)}, bf16[128,768]{1,0:T(8,128)(2,1)S(1)}, u32[]{:S(2)}, u32[]{:S(2)}) %collective-permute-start.7) | collective-permute-done | bytes 196640 | tf_op jit(solution)/shard_map/ppermute | solution.py:57
  63.6 1.5 %collective-permute-start.11 = (bf16[128,768]{1,0:T(8,128)(2,1)S(1)}, bf16[128,768]{1,0:T(8,128)(2,1)S(1)}, u32[]{:S(2)}, u32[]{:S(2)}) collective-permute-start(bf16[128,768]{1,0:T(8,128)(2,1)S(1)} %fusion.1), channel_id=1, source_target_pairs={{0,2},{1,3},{2,0},{3,1},{4,6},{5,7},{6,4},{7,5},{8,10},{9,11},{10,... | collective-permute-start | bytes 589832 | tf_op jit(solution)/shard_map/ppermute | solution.py:57
  65.1 2.4 %shard_map.71 = (bf16[4,128,1024]{2,1,0:T(8,128)(2,1)S(1)}, bf16[2,128,768]{2,1,0:T(8,128)(2,1)S(1)}, bf16[2,128,768]{2,1,0:T(8,128)(2,1)S(1)}) custom-call(bf16[144,1024]{1,0:T(8,128)(2,1)S(1)} %collective-permute-done.16.refs_0_, bf16[144,1024]{1,0:T(8,128)(2,1)S(1)} %collective-permute-done.15.refs_1_, bf16[4,768,1024]{2,1,0:T(8,128)(2,1)S(1)} %copy-done.1, ...), custom_call_target="tpu_custom_call" | custom-call | flops 2013265920 | bytes 15728640 | tf_op jit(solution)/shard_map/pallas_call | solution.py:154
  67.5 0.1 collective-permute-start.13
  67.6 0.5 collective-permute-start.17
  68.1 0.0 collective-permute-done.5.refs_7_
  68.1 5.8 %shard_map.72 = (bf16[4,768,1024]{2,1,0:T(8,128)(2,1)}, f32[8,128]{1,0:T(8,128)S(1)}) custom-call(bf16[2,128,768]{2,1,0:T(8,128)(2,1)S(1)} %get-tuple-element.31.refs_0_, bf16[2,128,768]{2,1,0:T(8,128)(2,1)S(1)} %collective-permute-done.refs_2_.refs_1_, bf16[2,128,768]{2,1,0:T(8,128)(2,1)S(1)} %collective-permute-done.1.refs_2_, ...), custom_call_target="tpu_custom_call" | custom-call | flops 8053063680 | bytes 15728640 | tf_op jit(solution)/shard_map/pallas_call | solution.py:256
  73.9 0.1 convert_add_fusion.1
  74.0 0.6 collective-permute-start.14
  74.6 0.1 convert_add_fusion
  74.7 1.6 %collective-permute-start.18 = (bf16[128,768]{1,0:T(8,128)(2,1)S(1)}, bf16[128,768]{1,0:T(8,128)(2,1)S(1)}, u32[]{:S(2)}, u32[]{:S(2)}) collective-permute-start(bf16[128,768]{1,0:T(8,128)(2,1)S(1)} %fusion.3), channel_id=1, source_target_pairs={{0,2},{1,3},{2,0},{3,1},{4,6},{5,7},{6,4},{7,5},{8,10},{9,11},{10,... | collective-permute-start | bytes 589832 | tf_op jit(solution)/shard_map/ppermute | solution.py:57
  76.3 5.5 %collective-permute-done.14.refs_13_ = bf16[128,768]{1,0:T(8,128)(2,1)S(1)} collective-permute-done((bf16[128,768]{1,0:T(8,128)(2,1)S(1)}, bf16[128,768]{1,0:T(8,128)(2,1)S(1)}, u32[]{:S(2)}, u32[]{:S(2)}) %collective-permute-start.14) | collective-permute-done | bytes 196640 | tf_op jit(solution)/shard_map/ppermute | solution.py:57
  81.8 3.4 %collective-permute-done.18.refs_15_ = bf16[128,768]{1,0:T(8,128)(2,1)S(1)} collective-permute-done((bf16[128,768]{1,0:T(8,128)(2,1)S(1)}, bf16[128,768]{1,0:T(8,128)(2,1)S(1)}, u32[]{:S(2)}, u32[]{:S(2)}) %collective-permute-start.18) | collective-permute-done | bytes 196640 | tf_op jit(solution)/shard_map/ppermute | solution.py:57
  85.2 0.4 shard_map.73
  85.6 0.1 collective-permute-start.21
  85.7 0.9 collective-permute-start.20
  86.5 1.0 %collective-permute-start.19 = (f32[4,768]{1,0:T(4,128)S(1)}, f32[4,768]{1,0:T(4,128)S(1)}, u32[]{:S(2)}, u32[]{:S(2)}) collective-permute-start(f32[4,768]{1,0:T(4,128)S(1)} %shard_map.73), channel_id=1, source_target_pairs={{0,1},{1,0},{2,3},{3,2},{4,5},{5,4},{6,7},{7,6},{8,9},{9,8},{10,11... | collective-permute-start | bytes 36872 | tf_op jit(solution)/shard_map/ppermute | solution.py:57
  87.5 1.3 %collective-permute-done.21 = f32[4,768]{1,0:T(4,128)S(1)} collective-permute-done((f32[4,768]{1,0:T(4,128)S(1)}, f32[4,768]{1,0:T(4,128)S(1)}, u32[]{:S(2)}, u32[]{:S(2)}) %collective-permute-start.21) | collective-permute-done | bytes 12320 | tf_op jit(solution)/shard_map/ppermute | solution.py:57
  88.8 0.7 collective-permute-done.20
  89.4 0.6 add_add_fusion
  (25 shorter events, 0.3 us)
Async XLA Ops:
  3.0 14.6 %collective-permute-start.9 = (bf16[144,1024]{1,0:T(8,128)(2,1)S(1)}, bf16[144,1024]{1,0:T(8,128)(2,1)S(1)}, u32[]{:S(2)}, u32[]{:S(2)}) collective-permute-start(bf16[144,1024]{1,0:T(8,128)(2,1)S(1)} %pad_maximum_fusion.refs_0_), channel_id=1, source_target_pairs={{0,4},{4,8},{8,12},{1,5},{5,9},{9,13},{2,6},{6,10},{10,14},{3,7},{... | collective-permute-start | bytes 884744 | tf_op jit(solution)/shard_map/ppermute | solution.py:35
  7.9 10.4 %collective-permute-start.8 = (bf16[144,1024]{1,0:T(8,128)(2,1)S(1)}, bf16[144,1024]{1,0:T(8,128)(2,1)S(1)}, u32[]{:S(2)}, u32[]{:S(2)}) collective-permute-start(bf16[144,1024]{1,0:T(8,128)(2,1)S(1)} %pad_maximum_fusion.refs_0_), channel_id=1, source_target_pairs={{4,0},{8,4},{12,8},{5,1},{9,5},{13,9},{6,2},{10,6},{14,10},{7,3},{... | collective-permute-start | bytes 884744 | tf_op jit(solution)/shard_map/ppermute | solution.py:35
  9.2 29.9 %collective-permute-start.15 = (bf16[144,1024]{1,0:T(8,128)(2,1)S(1)}, bf16[144,1024]{1,0:T(8,128)(2,1)S(1)}, u32[]{:S(2)}, u32[]{:S(2)}) collective-permute-start(bf16[144,1024]{1,0:T(8,128)(2,1)S(1)} %pad_maximum_fusion.refs_0_), channel_id=1, source_target_pairs={{0,8},{12,4},{1,9},{13,5},{2,10},{14,6},{3,11},{15,7},{16,24},{28,... | collective-permute-start | bytes 884744 | tf_op jit(solution)/shard_map/ppermute | solution.py:35
  16.0 51.5 %collective-permute-start.4 = (bf16[2,128,768]{2,1,0:T(8,128)(2,1)S(1)}, bf16[2,128,768]{2,1,0:T(8,128)(2,1)S(1)}, u32[]{:S(2)}, u32[]{:S(2)}) collective-permute-start(bf16[2,128,768]{2,1,0:T(8,128)(2,1)S(1)} %get-tuple-element.30.refs_4_), channel_id=1, source_target_pairs={{0,1},{1,0},{2,3},{3,2},{4,5},{5,4},{6,7},{7,6},{8,9},{9,8},{10,11... | collective-permute-start | bytes 1179656 | tf_op jit(solution)/shard_map/ppermute | solution.py:57
  16.1 25.8 %collective-permute-start.3 = (bf16[2,128,768]{2,1,0:T(8,128)(2,1)S(1)}, bf16[2,128,768]{2,1,0:T(8,128)(2,1)S(1)}, u32[]{:S(2)}, u32[]{:S(2)}) collective-permute-start(bf16[2,128,768]{2,1,0:T(8,128)(2,1)S(1)} %get-tuple-element.30.refs_4_), channel_id=1, source_target_pairs={{0,2},{1,3},{2,0},{3,1},{4,6},{5,7},{6,4},{7,5},{8,10},{9,11},{10,... | collective-permute-start | bytes 1179656 | tf_op jit(solution)/shard_map/ppermute | solution.py:57
  17.6 18.4 %collective-permute-start = (bf16[2,128,768]{2,1,0:T(8,128)(2,1)S(1)}, bf16[2,128,768]{2,1,0:T(8,128)(2,1)S(1)}, u32[]{:S(2)}, u32[]{:S(2)}) collective-permute-start(bf16[2,128,768]{2,1,0:T(8,128)(2,1)S(1)} %get-tuple-element.31.refs_0_), channel_id=1, source_target_pairs={{0,2},{1,3},{2,0},{3,1},{4,6},{5,7},{6,4},{7,5},{8,10},{9,11},{10,... | collective-permute-start | bytes 1179656 | tf_op jit(solution)/shard_map/ppermute | solution.py:57
  18.3 2.8 %copy-start = (bf16[4,768,1024]{2,1,0:T(8,128)(2,1)S(1)}, bf16[4,768,1024]{2,1,0:T(8,128)(2,1)}, u32[]{:S(2)}) copy-start(bf16[4,768,1024]{2,1,0:T(8,128)(2,1)} %refs_2_.5) | copy-start | bytes 18874372
  21.1 14.9 %copy-start.1 = (bf16[4,768,1024]{2,1,0:T(8,128)(2,1)S(1)}, bf16[4,768,1024]{2,1,0:T(8,128)(2,1)}, u32[]{:S(2)}) copy-start(bf16[4,768,1024]{2,1,0:T(8,128)(2,1)} %refs_2_.5) | copy-start | bytes 18874372
  23.5 14.9 %collective-permute-start.10 = (bf16[2,128,768]{2,1,0:T(8,128)(2,1)S(1)}, bf16[2,128,768]{2,1,0:T(8,128)(2,1)S(1)}, u32[]{:S(2)}, u32[]{:S(2)}) collective-permute-start(bf16[2,128,768]{2,1,0:T(8,128)(2,1)S(1)} %get-tuple-element.19), channel_id=1, source_target_pairs={{0,1},{1,0},{2,3},{3,2},{4,5},{5,4},{6,7},{7,6},{8,9},{9,8},{10,11... | collective-permute-start | bytes 1179656 | tf_op jit(solution)/shard_map/ppermute | solution.py:57
  36.0 31.6 %collective-permute-start.1 = (bf16[2,128,768]{2,1,0:T(8,128)(2,1)S(1)}, bf16[2,128,768]{2,1,0:T(8,128)(2,1)S(1)}, u32[]{:S(2)}, u32[]{:S(2)}) collective-permute-start(bf16[2,128,768]{2,1,0:T(8,128)(2,1)S(1)} %get-tuple-element.31.refs_0_), channel_id=1, source_target_pairs={{0,1},{1,0},{2,3},{3,2},{4,5},{5,4},{6,7},{7,6},{8,9},{9,8},{10,11... | collective-permute-start | bytes 1179656 | tf_op jit(solution)/shard_map/ppermute | solution.py:57
  38.4 2.0 %collective-permute-start.6 = (bf16[2,128,768]{2,1,0:T(8,128)(2,1)S(1)}, bf16[2,128,768]{2,1,0:T(8,128)(2,1)S(1)}, u32[]{:S(2)}, u32[]{:S(2)}) collective-permute-start(bf16[2,128,768]{2,1,0:T(8,128)(2,1)S(1)} %get-tuple-element.17), channel_id=1, source_target_pairs={{0,1},{1,0},{2,3},{3,2},{4,5},{5,4},{6,7},{7,6},{8,9},{9,8},{10,11... | collective-permute-start | bytes 1179656 | tf_op jit(solution)/shard_map/ppermute | solution.py:57
  39.1 17.2 %collective-permute-start.12 = (bf16[144,1024]{1,0:T(8,128)(2,1)S(1)}, bf16[144,1024]{1,0:T(8,128)(2,1)S(1)}, u32[]{:S(2)}, u32[]{:S(2)}) collective-permute-start(bf16[144,1024]{1,0:T(8,128)(2,1)S(1)} %broadcast_select_fusion), channel_id=1, source_target_pairs={{4,0},{8,12},{5,1},{9,13},{6,2},{10,14},{7,3},{11,15},{20,16},{24,... | collective-permute-start | bytes 884744 | tf_op jit(solution)/shard_map/ppermute | solution.py:35
  40.5 15.8 %collective-permute-start.16 = (bf16[144,1024]{1,0:T(8,128)(2,1)S(1)}, bf16[144,1024]{1,0:T(8,128)(2,1)S(1)}, u32[]{:S(2)}, u32[]{:S(2)}) collective-permute-start(bf16[144,1024]{1,0:T(8,128)(2,1)S(1)} %collective-permute-done.15.refs_1_), channel_id=1, source_target_pairs={{4,0},{8,12},{5,1},{9,13},{6,2},{10,14},{7,3},{11,15},{20,16},{24,... | collective-permute-start | bytes 884744 | tf_op jit(solution)/shard_map/ppermute | solution.py:35
  41.9 26.2 %collective-permute-start.2 = (bf16[2,128,768]{2,1,0:T(8,128)(2,1)S(1)}, bf16[2,128,768]{2,1,0:T(8,128)(2,1)S(1)}, u32[]{:S(2)}, u32[]{:S(2)}) collective-permute-start(bf16[2,128,768]{2,1,0:T(8,128)(2,1)S(1)} %collective-permute-done.refs_2_.refs_1_), channel_id=1, source_target_pairs={{0,1},{1,0},{2,3},{3,2},{4,5},{5,4},{6,7},{7,6},{8,9},{9,8},{10,11... | collective-permute-start | bytes 1179656 | tf_op jit(solution)/shard_map/ppermute | solution.py:57
  56.3 11.8 %collective-permute-start.5 = (bf16[2,128,768]{2,1,0:T(8,128)(2,1)S(1)}, bf16[2,128,768]{2,1,0:T(8,128)(2,1)S(1)}, u32[]{:S(2)}, u32[]{:S(2)}) collective-permute-start(bf16[2,128,768]{2,1,0:T(8,128)(2,1)S(1)} %collective-permute-done.3.refs_5_), channel_id=1, source_target_pairs={{0,1},{1,0},{2,3},{3,2},{4,5},{5,4},{6,7},{7,6},{8,9},{9,8},{10,11... | collective-permute-start | bytes 1179656 | tf_op jit(solution)/shard_map/ppermute | solution.py:57
  56.3 7.3 %collective-permute-start.7 = (bf16[128,768]{1,0:T(8,128)(2,1)S(1)}, bf16[128,768]{1,0:T(8,128)(2,1)S(1)}, u32[]{:S(2)}, u32[]{:S(2)}) collective-permute-start(bf16[128,768]{1,0:T(8,128)(2,1)S(1)} %fusion), channel_id=1, source_target_pairs={{0,2},{1,3},{2,0},{3,1},{4,6},{5,7},{6,4},{7,5},{8,10},{9,11},{10,... | collective-permute-start | bytes 589832 | tf_op jit(solution)/shard_map/ppermute | solution.py:57
  63.6 12.7 %collective-permute-start.11 = (bf16[128,768]{1,0:T(8,128)(2,1)S(1)}, bf16[128,768]{1,0:T(8,128)(2,1)S(1)}, u32[]{:S(2)}, u32[]{:S(2)}) collective-permute-start(bf16[128,768]{1,0:T(8,128)(2,1)S(1)} %fusion.1), channel_id=1, source_target_pairs={{0,2},{1,3},{2,0},{3,1},{4,6},{5,7},{6,4},{7,5},{8,10},{9,11},{10,... | collective-permute-start | bytes 589832 | tf_op jit(solution)/shard_map/ppermute | solution.py:57
  67.5 6.4 %collective-permute-start.13 = (bf16[2,128,768]{2,1,0:T(8,128)(2,1)S(1)}, bf16[2,128,768]{2,1,0:T(8,128)(2,1)S(1)}, u32[]{:S(2)}, u32[]{:S(2)}) collective-permute-start(bf16[2,128,768]{2,1,0:T(8,128)(2,1)S(1)} %get-tuple-element.21), channel_id=1, source_target_pairs={{0,1},{1,0},{2,3},{3,2},{4,5},{5,4},{6,7},{7,6},{8,9},{9,8},{10,11... | collective-permute-start | bytes 1179656 | tf_op jit(solution)/shard_map/ppermute | solution.py:57
  67.6 7.0 %collective-permute-start.17 = (bf16[2,128,768]{2,1,0:T(8,128)(2,1)S(1)}, bf16[2,128,768]{2,1,0:T(8,128)(2,1)S(1)}, u32[]{:S(2)}, u32[]{:S(2)}) collective-permute-start(bf16[2,128,768]{2,1,0:T(8,128)(2,1)S(1)} %get-tuple-element.23), channel_id=1, source_target_pairs={{0,1},{1,0},{2,3},{3,2},{4,5},{5,4},{6,7},{7,6},{8,9},{9,8},{10,11... | collective-permute-start | bytes 1179656 | tf_op jit(solution)/shard_map/ppermute | solution.py:57
  74.0 7.8 %collective-permute-start.14 = (bf16[128,768]{1,0:T(8,128)(2,1)S(1)}, bf16[128,768]{1,0:T(8,128)(2,1)S(1)}, u32[]{:S(2)}, u32[]{:S(2)}) collective-permute-start(bf16[128,768]{1,0:T(8,128)(2,1)S(1)} %fusion.2), channel_id=1, source_target_pairs={{0,2},{1,3},{2,0},{3,1},{4,6},{5,7},{6,4},{7,5},{8,10},{9,11},{10,... | collective-permute-start | bytes 589832 | tf_op jit(solution)/shard_map/ppermute | solution.py:57
  74.7 10.4 %collective-permute-start.18 = (bf16[128,768]{1,0:T(8,128)(2,1)S(1)}, bf16[128,768]{1,0:T(8,128)(2,1)S(1)}, u32[]{:S(2)}, u32[]{:S(2)}) collective-permute-start(bf16[128,768]{1,0:T(8,128)(2,1)S(1)} %fusion.3), channel_id=1, source_target_pairs={{0,2},{1,3},{2,0},{3,1},{4,6},{5,7},{6,4},{7,5},{8,10},{9,11},{10,... | collective-permute-start | bytes 589832 | tf_op jit(solution)/shard_map/ppermute | solution.py:57
  85.6 3.2 %collective-permute-start.21 = (f32[4,768]{1,0:T(4,128)S(1)}, f32[4,768]{1,0:T(4,128)S(1)}, u32[]{:S(2)}, u32[]{:S(2)}) collective-permute-start(f32[4,768]{1,0:T(4,128)S(1)} %shard_map.73), channel_id=1, source_target_pairs={{0,3},{1,2},{2,1},{3,0},{4,7},{5,6},{6,5},{7,4},{8,11},{9,10},{10,... | collective-permute-start | bytes 36872 | tf_op jit(solution)/shard_map/ppermute | solution.py:57
  85.7 3.8 %collective-permute-start.20 = (f32[4,768]{1,0:T(4,128)S(1)}, f32[4,768]{1,0:T(4,128)S(1)}, u32[]{:S(2)}, u32[]{:S(2)}) collective-permute-start(f32[4,768]{1,0:T(4,128)S(1)} %shard_map.73), channel_id=1, source_target_pairs={{0,2},{1,3},{2,0},{3,1},{4,6},{5,7},{6,4},{7,5},{8,10},{9,11},{10,... | collective-permute-start | bytes 36872 | tf_op jit(solution)/shard_map/ppermute | solution.py:57
  86.5 2.9 %collective-permute-start.19 = (f32[4,768]{1,0:T(4,128)S(1)}, f32[4,768]{1,0:T(4,128)S(1)}, u32[]{:S(2)}, u32[]{:S(2)}) collective-permute-start(f32[4,768]{1,0:T(4,128)S(1)} %shard_map.73), channel_id=1, source_target_pairs={{0,1},{1,0},{2,3},{3,2},{4,5},{5,4},{6,7},{7,6},{8,9},{9,8},{10,11... | collective-permute-start | bytes 36872 | tf_op jit(solution)/shard_map/ppermute | solution.py:57
